TPU v7x, 512 devices: a whole 4x4x16 slice. The times are simulated.
512 devices in a mesh: ctx: 16 (over z), head: 32 (over x, y, core).
Axes of the slice: x: 4, y: 4, z: 16, core: 2. Of those that a mesh axis runs over, the one named last changes fastest.
Arguments:
- mixer_input: bfloat16 [8192, 8192], P('ctx', 'head')
- gate_input: bfloat16 [8192, 8192], P('ctx', 'head'), may hold values from -6 to 6
- step_raw: float32 [8192, 128], P('ctx', 'head'), may hold values from -16 to 4
- decay_log: float32 [128], P('head'), may hold values from -1.39 to -0.28
- skip_weight: float32 [128], P('head'), may hold values from 0.5 to 1.5
- state_maps: bfloat16 [8192, 2, 8, 128], P('ctx'), may hold values from -6 to 6
- norm_gain: float32 [8192], P('head'), may hold values from 0.25 to 1.75
- queries: bfloat16 [8192, 8192], P('ctx', 'head')
- keys_values: bfloat16 [8192, 2, 8, 128], P('ctx')
Outputs:
- mamba_out: bfloat16 [8192, 8192], P('ctx', 'head')
- attn_out: bfloat16 [8192, 8192], P('ctx', 'head')
All inputs are finite; a program needn't handle non-finite values.
Results may differ from a plain program's by a relative error of at most 0.017.
Values may be sent and summed in bfloat16 or wider, within the bound.
A program may use at most 64 MiB of HBM per device.

v0:
```python
import jax
import jax.numpy as jnp
from jax import lax
from jax.sharding import PartitionSpec as P

SPAN = 128


NEG_FILL = -1e30
EPSILON = 1e-05


def carried_in(value, axis, combine, identity):
    size, place = (lax.axis_size(axis), lax.axis_index(axis))
    everything = jax.tree.map(
        lambda part, kind: lax.all_gather(part.astype(kind), axis),
        value,
        (jnp.bfloat16, jnp.bfloat16),
    )
    start = jax.tree.map(
        lambda part, zero: jnp.broadcast_to(jnp.asarray(zero, part.dtype), part.shape),
        value,
        identity,
    )

    def turn(k, before):
        reached = k < place
        new = combine(
            before, jax.tree.map(lambda part, own: part[k].astype(own.dtype), everything, value)
        )
        return jax.tree.map(lambda a, b: jnp.where(reached, a, b), new, before)

    return lax.fori_loop(0, size, turn, start)


def span_pass(x_rows, dt_rows, decay_rate, b_rows, c_rows, span_len):
    length, head_count, head_width = x_rows.shape
    block_count = length // span_len
    logs_rows = dt_rows * decay_rate[None, :]
    offsets = jnp.arange(span_len)
    below_diag = offsets[:, None] >= offsets[None, :]

    def advance(running, inputs):
        x_block, dt_block, log_block, b_block, c_block = inputs
        cumulative = jnp.cumsum(log_block, axis=0)
        cumul_heads = cumulative.T
        spread = jnp.where(
            below_diag[None], cumul_heads[:, :, None] - cumul_heads[:, None, :], NEG_FILL
        )
        scores = jnp.dot(c_block, b_block.T, preferred_element_type=jnp.float32)
        weights = (scores[None] * jnp.exp(spread) * dt_block.T[:, None, :]).astype(jnp.bfloat16)
        inside = jnp.einsum("hts,shp->thp", weights, x_block, preferred_element_type=jnp.float32)
        carried = jnp.einsum(
            "tn,hnp->thp", c_block.astype(jnp.float32), running, precision=lax.Precision.HIGHEST
        )
        carried = carried * jnp.exp(cumulative)[:, :, None]
        tail_decay = jnp.exp(cumulative[-1][None, :] - cumulative) * dt_block
        state_loads = (tail_decay.T[:, :, None] * b_block.astype(jnp.float32)[None, :, :]).astype(
            jnp.bfloat16
        )
        fresh_state = jnp.einsum(
            "hsn,shp->hnp", state_loads, x_block, preferred_element_type=jnp.float32
        )
        running = jnp.exp(cumulative[-1])[:, None, None] * running + fresh_state
        return (running, inside + carried)

    blocks = (
        x_rows.reshape(block_count, span_len, head_count, head_width),
        dt_rows.reshape(block_count, span_len, head_count),
        logs_rows.reshape(block_count, span_len, head_count),
        b_rows.reshape(block_count, span_len, b_rows.shape[1]),
        c_rows.reshape(block_count, span_len, c_rows.shape[1]),
    )
    starting = jnp.zeros((head_count, b_rows.shape[1], head_width), jnp.float32)
    final_state, outputs = lax.scan(advance, starting, blocks)
    return (outputs.reshape(length, head_count, head_width), final_state)


def slot_positions(device, offsets, half_len):
    first_pos = 2 * device * half_len + offsets
    second = (2 * device + 1) * half_len + offsets
    return (first_pos, second)


def attend_block(slot_state, query_mat, query_pos, key_block, key_pos):
    maxima, totals, accumulated = slot_state
    head_dim = key_block.shape[1] // 2
    key_mat = key_block[:, :head_dim]
    value_mat = key_block[:, head_dim:]
    scores = jnp.einsum(
        "qhd,kd->qhk", query_mat, key_mat, preferred_element_type=jnp.float32
    ) * head_dim ** (-0.5)
    visible = (query_pos[:, None] >= key_pos[None, :])[:, None, :]
    scores = jnp.where(visible, scores, NEG_FILL)
    new_max = jnp.maximum(maxima, jnp.max(scores, axis=2))
    weights = jnp.where(visible, jnp.exp(scores - new_max[:, :, None]), 0.0)
    rescale = jnp.exp(maxima - new_max)
    totals = totals * rescale + jnp.sum(weights, axis=2)
    accumulated = accumulated * rescale[:, :, None] + jnp.einsum(
        "qhk,kd->qhd", weights.astype(jnp.bfloat16), value_mat, preferred_element_type=jnp.float32
    )
    return (new_max, totals, accumulated)


def attend_slot(slot_state, query_mat, query_pos, key_rows, key_pos):
    key_count = key_rows.shape[0]
    block_len = 1024
    key_blocks = key_rows.reshape(key_count // block_len, block_len, key_rows.shape[1])
    pos_blocks = key_pos.reshape(key_count // block_len, block_len)
    top_query = jnp.max(query_pos)

    def visit(running, inputs):
        key_block, block_pos = inputs
        skipped = jnp.min(block_pos) > top_query
        running = lax.cond(
            skipped,
            lambda current: current,
            lambda current: attend_block(current, query_mat, query_pos, key_block, block_pos),
            running,
        )
        return (running, None)

    slot_state, unused = lax.scan(visit, slot_state, (key_blocks, pos_blocks))
    return slot_state


def body(
    mixer_input,
    gate_input,
    step_raw,
    decay_log,
    skip_weight,
    state_maps,
    norm_gain,
    queries,
    keys_values,
):
    row_count = mixer_input.shape[0]
    head_count = decay_log.shape[0]
    head_width = mixer_input.shape[1] // head_count
    group_count = state_maps.shape[2]
    per_group = head_count * lax.axis_size("head") // group_count
    group_index = lax.axis_index("head") * head_count // per_group
    ctx_index = lax.axis_index("ctx")
    group_maps = lax.dynamic_index_in_dim(state_maps, group_index, axis=2, keepdims=False)
    b_rows = group_maps[:, 0]
    c_rows = group_maps[:, 1]
    x_rows = mixer_input.reshape(row_count, head_count, head_width)
    decay_rate = -jnp.exp(decay_log)
    dt_rows = jax.nn.softplus(step_raw)
    local_mixed, local_state = span_pass(x_rows, dt_rows, decay_rate, b_rows, c_rows, SPAN)
    cumulative = jnp.cumsum(dt_rows * decay_rate[None, :], axis=0)
    total_log = cumulative[-1]

    def combine(earlier, following):
        return (
            earlier[0] + following[0],
            jnp.exp(following[0])[:, None, None] * earlier[1] + following[1],
        )

    identity = (jnp.zeros_like(total_log), jnp.zeros_like(local_state))
    entering = carried_in((total_log, local_state), "ctx", combine, identity)[1]
    carried = jnp.einsum(
        "tn,hnp->thp", c_rows.astype(jnp.float32), entering, precision=lax.Precision.HIGHEST
    )
    mixed = local_mixed + carried * jnp.exp(cumulative)[:, :, None]
    mixed = mixed + skip_weight[None, :, None] * x_rows.astype(jnp.float32)
    gated = mixed * jax.nn.silu(
        gate_input.reshape(row_count, head_count, head_width).astype(jnp.float32)
    )
    squares = jnp.sum(gated * gated, axis=(1, 2))
    selector = (jnp.arange(group_count, dtype=jnp.int32) == group_index).astype(jnp.float32)
    group_sums = lax.psum(squares[:, None] * selector[None, :], "head")
    mean_square = jnp.sum(group_sums * selector[None, :], axis=1) / (per_group * head_width)
    normed = gated * lax.rsqrt(mean_square + EPSILON)[:, None, None]
    mamba_out = (normed.reshape(row_count, -1) * norm_gain[None, :]).astype(jnp.bfloat16)
    head_dim = keys_values.shape[3]
    q_heads = queries.shape[1] // head_dim
    kv_groups = keys_values.shape[2]
    per_kv = q_heads * lax.axis_size("head") // kv_groups
    kv_index = lax.axis_index("head") * q_heads // per_kv
    kv_pairs = lax.dynamic_index_in_dim(keys_values, kv_index, axis=2, keepdims=False).reshape(
        row_count, 2 * head_dim
    )
    half_len = row_count // 2
    query_width = queries.shape[1]
    query_slots = queries.reshape(2, half_len, query_width)
    pair_slots = kv_pairs.reshape(2, half_len, 2 * head_dim)
    query_offsets = jnp.arange(half_len, dtype=jnp.int32)
    query_first, query_second = slot_positions(ctx_index, query_offsets, half_len)
    query_places = (query_first, query_second)
    query_mats = [
        query_slots[slot_index].reshape(half_len, q_heads, head_dim) for slot_index in range(2)
    ]
    starting = (
        jnp.full((2, half_len, q_heads), NEG_FILL, jnp.float32),
        jnp.zeros((2, half_len, q_heads), jnp.float32),
        jnp.zeros((2, half_len, q_heads, head_dim), jnp.float32),
    )
    shard_rows = lax.all_gather(pair_slots, "ctx", axis=1, tiled=True)
    key_count = shard_rows.shape[1]
    row_ids = jnp.arange(key_count, dtype=jnp.int32)
    devices = row_ids // half_len
    key_first, key_second = slot_positions(devices, row_ids % half_len, half_len)
    key_places = (key_first, key_second)
    updated = []
    for slot_index in range(2):
        slot_state = (starting[0][slot_index], starting[1][slot_index], starting[2][slot_index])
        for key_slot in range(2):
            slot_state = attend_slot(
                slot_state,
                query_mats[slot_index],
                query_places[slot_index],
                shard_rows[key_slot],
                key_places[key_slot],
            )
        updated.append(slot_state)
    maxima, totals, accumulated = tuple(
        (jnp.stack([slot_entry[member] for slot_entry in updated]) for member in range(3))
    )
    results = (
        (accumulated / totals[:, :, :, None]).astype(jnp.bfloat16).reshape(2, half_len, query_width)
    )
    attn_out = results.reshape(row_count, query_width)
    return (mamba_out, attn_out)


def solution(mesh):
    in_specs = (
        P("ctx", "head"),
        P("ctx", "head"),
        P("ctx", "head"),
        P("head"),
        P("head"),
        P("ctx", None, None, None),
        P("head"),
        P("ctx", "head"),
        P("ctx", None, None, None),
    )
    out_specs = (P("ctx", "head"), P("ctx", "head"))
    return jax.shard_map(body, mesh=mesh, in_specs=in_specs, out_specs=out_specs, check_vma=False)
```

profile of v0, /device:TPU:480, one launch (start us, length us, event | category | flops | bytes accessed | tf_op | source)
XLA Modules:
  0.0 364.9 jit_solution(12090021142076644944)
XLA Ops:
  7.3 1.5 copy-done
  11.1 1.2 reshape.239
  13.3 39.9 %while.91 = (s32[]{:T(128)}, f32[4,128,64]{1,2,0:T(8,128)S(1)}, f32[4,128,4,64]{1,0,3,2:T(4,128)}, f32[4,128,4]{2,1,0:T(8,128)}, f32[4,128,4]{2,1,0:T(8,128)S(1)...) while((s32[]{:T(128)}, f32[4,128,64]{1,2,0:T(8,128)S(1)}, ...), condition=%wide.region_2.3_spmd.clone, body=%wide.region_0.2_spmd.clone.sunk | while | flops 72024576 | bytes 1917167 | solution.py:75
  15.8 1.1 fusion.138
  16.9 4.4 %dynamic_update_slice.6 = f32[4,128,4,64]{1,0,3,2:T(4,128)} dynamic-update-slice(f32[4,128,4,64]{1,0,3,2:T(4,128)} %get-tuple-element.1393, f32[1,128,4,64]{1,0,3,2:T(1,128)S(1)} %bitcast.230, s32[]{:T(128)} %get-tuple-element.1391, s32[]{:T(128)} %constant.237.clone.1..sunk, s32[]{:T(128)} %constant.237.clone.1..sunk, s32[]{:T(128)} %constant.237.clone.1..sunk) | dynamic-update-slice | bytes 262148 | tf_op jit(solution)/shard_map/while/body/jit(dynamic_update_index_in_dim)/dynamic_update_slice | solution.py:75
  22.2 1.1 convolution_add_fusion.6
  25.8 1.1 fusion.138
  26.9 4.4 %dynamic_update_slice.6 = f32[4,128,4,64]{1,0,3,2:T(4,128)} dynamic-update-slice(f32[4,128,4,64]{1,0,3,2:T(4,128)} %get-tuple-element.1393, f32[1,128,4,64]{1,0,3,2:T(1,128)S(1)} %bitcast.230, s32[]{:T(128)} %get-tuple-element.1391, s32[]{:T(128)} %constant.237.clone.1..sunk, s32[]{:T(128)} %constant.237.clone.1..sunk, s32[]{:T(128)} %constant.237.clone.1..sunk) | dynamic-update-slice | bytes 262148 | tf_op jit(solution)/shard_map/while/body/jit(dynamic_update_index_in_dim)/dynamic_update_slice | solution.py:75
  32.2 1.1 convolution_add_fusion.6
  35.8 1.1 fusion.138
  36.9 4.4 %dynamic_update_slice.6 = f32[4,128,4,64]{1,0,3,2:T(4,128)} dynamic-update-slice(f32[4,128,4,64]{1,0,3,2:T(4,128)} %get-tuple-element.1393, f32[1,128,4,64]{1,0,3,2:T(1,128)S(1)} %bitcast.230, s32[]{:T(128)} %get-tuple-element.1391, s32[]{:T(128)} %constant.237.clone.1..sunk, s32[]{:T(128)} %constant.237.clone.1..sunk, s32[]{:T(128)} %constant.237.clone.1..sunk) | dynamic-update-slice | bytes 262148 | tf_op jit(solution)/shard_map/while/body/jit(dynamic_update_index_in_dim)/dynamic_update_slice | solution.py:75
  42.1 1.1 convolution_add_fusion.6
  45.8 1.1 fusion.138
  46.9 4.4 %dynamic_update_slice.6 = f32[4,128,4,64]{1,0,3,2:T(4,128)} dynamic-update-slice(f32[4,128,4,64]{1,0,3,2:T(4,128)} %get-tuple-element.1393, f32[1,128,4,64]{1,0,3,2:T(1,128)S(1)} %bitcast.230, s32[]{:T(128)} %get-tuple-element.1391, s32[]{:T(128)} %constant.237.clone.1..sunk, s32[]{:T(128)} %constant.237.clone.1..sunk, s32[]{:T(128)} %constant.237.clone.1..sunk) | dynamic-update-slice | bytes 262148 | tf_op jit(solution)/shard_map/while/body/jit(dynamic_update_index_in_dim)/dynamic_update_slice | solution.py:75
  52.1 1.1 convolution_add_fusion.6
  54.0 3.5 dynamic-slice_reduce_fusion
  58.4 1.1 copy.113
  60.3 1.6 fusion.100
  61.9 1.0 copy.133
  64.6 1.2 reduce-window.6
  66.4 25.5 %all-gather.1 = bf16[16,1,4]{2,1,0:T(2,128)(2,1)S(1)} all-gather(bf16[1,1,4]{2,1,0:T(2,128)(2,1)S(1)} %slice_bitcast_fusion.17), channel_id=1, replica_groups=mesh['ctx'=16,'head'=32] {'ctx'}, dimensions={0}, use_global_device_ids=true | all-gather | bytes 136 | tf_op jit(solution)/shard_map/all_gather | solution.py:16
  92.1 2.1 reshape.214
  94.2 1.9 copy.114
  96.1 26.5 %all-gather.7.cloned.1.call-done = bf16[64,128,64]{1,2,0:T(8,128)(2,1)} async-done(((bf16[4,128,64]{1,2,0:T(8,128)(2,1)}), bf16[64,128,64]{1,2,0:T(8,128)(2,1)}) %all-gather.7.cloned.1.call-update) | async-done | bytes 1048592 | tf_op jit(solution)/shard_map/all_gather | solution.py:16
  122.7 18.2 %while.92 = (s32[]{:T(128)}, f32[4,128,64]{2,1,0:T(8,128)S(1)}, s32[]{:T(128)}, bf16[16,4]{1,0:T(8,128)(2,1)S(1)}, bf16[16,4,128,64]{2,3,1,0:T(8,128)(2,1)}, /*index=5*/s32[]{:T(128)}, s32[]{:T(128)}) while((s32[]{:T(128)}, f32[4,128,64]{2,1,0:T(8,128)S(1)}, s32[]{:T(128)}, bf16[16,4]{1,0:T(8,128)(2,1)S(1)}, ...), condition=%wide.region_6.7_spmd.clone, body=%wide.region_5.6_spmd.clone.sunk | while | flops 163848 | bytes 589969 | solution.py:33
  141.4 1.5 multiply_reduce_fusion
  142.9 123.9 %psum.7 = f32[512,8]{0,1:T(8,128)S(1)} all-reduce(f32[512,8]{0,1:T(8,128)S(1)} %broadcast_multiply_fusion.1), channel_id=1, replica_groups=mesh['ctx'=16,'head'=32] {'head'}, use_global_device_ids=true, to_apply=%region_8.9 | all-reduce | flops 4096 | bytes 32768 | tf_op jit(solution)/shard_map/psum | solution.py:173
  268.0 4.5 %fusion.99 = (bf16[1,4096,256]{2,1,0:T(8,128)(2,1)}, bf16[1,4096,256]{2,1,0:T(8,128)(2,1)}) fusion(bf16[2,4096,256]{2,1,0:T(8,128)(2,1)} %all-gather.5.cloned.1.call-done), kind=kLoop, calls=%fused_computation.181 | loop fusion | bytes 8388608 | tf_op jit(solution)/shard_map/slice | solution.py:214
  272.5 21.2 %while.87 = (s32[]{:T(128)}, f32[256,2]{0,1:T(2,128)S(1)}, f32[256,2]{0,1:T(2,128)S(1)}, f32[256,2,128]{2,0,1:T(8,128)S(1)}, s32[4,1024]{1,0:T(4,128)S(1)}, /*in...) while((s32[]{:T(128)}, f32[256,2]{0,1:T(2,128)S(1)}, ...), condition=%wide.region_17.18_spmd.clone, body=%wide.region_11.17_spmd.clone.sunk | while | flops 275646720 | bytes 9617659 | solution.py:123
  274.5 3.3 conditional.12
  274.8 1.1 dynamic-slice_bitcast_fusion
  279.8 3.3 conditional.12
  280.1 1.1 dynamic-slice_bitcast_fusion
  285.1 3.3 conditional.12
  285.4 1.1 dynamic-slice_bitcast_fusion
  290.4 3.3 conditional.12
  290.7 1.1 dynamic-slice_bitcast_fusion
  293.7 21.2 %while.88 = (s32[]{:T(128)}, f32[256,2]{0,1:T(2,128)S(1)}, f32[256,2]{0,1:T(2,128)S(1)}, f32[256,2,128]{2,0,1:T(8,128)S(1)}, s32[4,1024]{1,0:T(4,128)S(1)}, /*in...) while((s32[]{:T(128)}, f32[256,2]{0,1:T(2,128)S(1)}, ...), condition=%wide.region_24.25_spmd.clone, body=%wide.region_18.24_spmd.clone.sunk | while | flops 275646720 | bytes 9617659 | solution.py:123
  295.7 3.3 conditional.13
  296.0 1.1 dynamic-slice_bitcast_fusion.1
  301.0 3.3 conditional.13
  301.3 1.1 dynamic-slice_bitcast_fusion.1
  306.3 3.3 conditional.13
  306.6 1.1 dynamic-slice_bitcast_fusion.1
  311.6 3.3 conditional.13
  311.9 1.1 dynamic-slice_bitcast_fusion.1
  315.0 20.9 %while.89 = (s32[]{:T(128)}, f32[256,2]{0,1:T(2,128)S(1)}, f32[256,2]{0,1:T(2,128)S(1)}, f32[256,2,128]{2,0,1:T(8,128)S(1)}, s32[4,1024]{1,0:T(4,128)S(1)}, /*in...) while((s32[]{:T(128)}, f32[256,2]{0,1:T(2,128)S(1)}, ...), condition=%wide.region_32.33_spmd.clone, body=%wide.region_26.32_spmd.clone.sunk | while | flops 275646720 | bytes 9617659 | solution.py:123
  316.9 3.3 conditional.14
  317.2 1.1 dynamic-slice_bitcast_fusion.2
  322.1 3.3 conditional.14
  322.4 1.1 dynamic-slice_bitcast_fusion.2
  327.4 3.3 conditional.14
  327.6 1.1 dynamic-slice_bitcast_fusion.2
  332.6 3.3 conditional.14
  332.8 1.1 dynamic-slice_bitcast_fusion.2
  335.9 20.9 %while.90 = (s32[]{:T(128)}, f32[256,2]{0,1:T(2,128)S(1)}, f32[256,2]{0,1:T(2,128)S(1)}, f32[256,2,128]{2,0,1:T(8,128)S(1)}, s32[4,1024]{1,0:T(4,128)S(1)}, /*in...) while((s32[]{:T(128)}, f32[256,2]{0,1:T(2,128)S(1)}, ...), condition=%wide.region_39.40_spmd.clone, body=%wide.region_33.39_spmd.clone.sunk | while | flops 275646720 | bytes 9617659 | solution.py:123
  337.8 3.3 conditional.15
  338.1 1.1 dynamic-slice_bitcast_fusion.3
  343.1 3.3 conditional.15
  343.3 1.1 dynamic-slice_bitcast_fusion.3
  348.3 3.3 conditional.15
  348.6 1.1 dynamic-slice_bitcast_fusion.3
  353.5 3.3 conditional.15
  353.8 1.1 dynamic-slice_bitcast_fusion.3
  (344 shorter events, 86.7 us)
Async XLA Ops:
  7.2 1.6 copy-start
  7.2 2.8 copy-start.5
  7.2 2.8 copy-start.2
  7.2 115.5 %all-gather.7.cloned.1.call-start = ((), (), s32[]{:S(2)}) async-start(), calls=%async_computation.1 | async-start | bytes 1114112 | tf_op jit(solution)/shard_map/all_gather | solution.py:16
  53.9 214.1 %all-gather.5.cloned.1.call-start = ((), (), s32[]{:S(2)}) async-start(), calls=%async_computation | async-start | bytes 4456448 | tf_op jit(solution)/shard_map/all_gather | solution.py:200
  122.7 18.7 %copy-start.4 = (f32[4]{0:T(128)S(1)}, f32[4]{0:T(128)}, u32[]{:S(2)}) copy-start(f32[4]{0:T(128)} %param.33) | copy-start | bytes 52
  141.4 125.9 %copy-start.3 = (f32[256]{0:T(256)S(1)}, f32[256]{0:T(256)}, u32[]{:S(2)}) copy-start(f32[256]{0:T(256)} %param.35) | copy-start | bytes 3076
  268.0 4.5 %copy-start.1 = (bf16[256,2,128]{2,0,1:T(8,128)(2,1)S(1)}, bf16[256,2,128]{2,0,1:T(8,128)(2,1)}, u32[]{:S(2)}) copy-start(bf16[256,2,128]{2,0,1:T(8,128)(2,1)} %copy.117) | copy-start | bytes 393220
Sparse Core Ops, SparseCore 0:
  54.0 68.5 all-gather.6
  125.3 75.7 all-gather.4
where the time goes:
time: 368 us; the launch traced here: 365 us
  blocking collectives  149 us (40%)
  local copies, waits for them, and re-layouts  80.4 us (22%)
  other arithmetic  35.6 us (10%)
  matrix products  35.3 us (10%)
  waiting for transfers between devices  26.6 us (7%)
  loops' own time  23.1 us (6%)
  between operations  14.4 us (4%)
    psum x1, blocking collectives, body(): group_sums = lax.psum(squares[:, None] * selector[None, :], 'head')  124 us
    all_gather x1, waiting for transfers between devices, carried_in(): lax.all_gather(part.astype(kind), axis)  26.5 us
    all_gather x1, blocking collectives, carried_in(): lax.all_gather(part.astype(kind), axis)  25.5 us
    another operation x4, loops' own time, attend_slot(): slot_state, unused = lax.scan(visit, slot_state, (key_blocks, pos_blocks))  21.4 us
    dynamic_update_slice x4, local copies, waits for them, and re-layouts, span_pass(): final_state, outputs = lax.scan(advance, starting, blocks)  17.5 us
    squeeze x16, local copies, waits for them, and re-layouts, attend_slot(): slot_state, unused = lax.scan(visit, slot_state, (key_blocks, pos_blocks))  17.3 us
    dynamic_slice x32, local copies, waits for them, and re-layouts, turn(): part[k].astype(own.dtype)  15.7 us
    dot_general x16, matrix products, attend_block(): jnp.einsum('qhk,kd->qhd', weights.astype(jnp.bfloat16), value_mat, prefer...  14.1 us
  transfers between devices with their start and end apart: 2, of which 1 were waited for; matrix products, arithmetic and copies ran while one was open for 10% of the time, Pallas kernels for 0%

commit v1 on v0

v1 whole, which is shorter than its diff:
```python
import functools
import math

import jax
import jax.numpy as jnp
from jax import lax
from jax.experimental import pallas as pl
from jax.experimental.pallas import tpu as pltpu
from jax.sharding import PartitionSpec as P

MESH = pl.DeviceIdType.MESH
HIGH = lax.Precision.HIGHEST
NEG_FILL = -1e30
EPSILON = 1e-5
SPAN = 128
CHUNKS = 4
UP = 8
DOWN = 7
M4_STEP = 4
M5_STEP = 7


def softplus(v):
    u = jnp.exp(-jnp.abs(v))
    small = u * (1.0 - u * (0.5 - u * (1.0 / 3.0 - u * 0.25)))
    return jnp.maximum(v, 0.0) + jnp.where(u < 0.02, small, jnp.log(1.0 + u))


def silu(v):
    return v / (1.0 + jnp.exp(-v))


def dot(a, b, **kw):
    return jnp.dot(a, b, preferred_element_type=jnp.float32, **kw)


def dot_t(a, b, **kw):
    return lax.dot_general(
        a, b, (((1,), (1,)), ((), ())), preferred_element_type=jnp.float32, **kw
    )


def kernel(
    n_ctx,
    decay_ref,
    skip_ref,
    step_ref,
    x_ref,
    gate_ref,
    maps_ref,
    gain_ref,
    q_ref,
    kv_ref,
    mamba_ref,
    attn_ref,
    kvbuf,
    qt,
    m_run,
    l_run,
    acc,
    mixed,
    decay_t,
    gated,
    total_buf,
    sbuf,
    srecv,
    ebuf,
    erecv,
    sq_buf,
    up_send,
    up_recv,
    dn_send,
    dn_recv,
    sib_send,
    sib_recv,
    sibd_send,
    sibd_recv,
    d_send,
    d_recv,
    s_send,
    s_recv,
    e_send,
    e_recv,
    q_send,
    q_recv,
):
    z = lax.axis_index("ctx")
    hd = lax.axis_index("head")
    core = lax.rem(hd, 2)
    sib = hd + 1 - 2 * core
    base = hd - lax.rem(hd, 4)
    place = lax.rem(hd, 4)
    above = lax.rem(z + 1, n_ctx)
    below = lax.rem(z + n_ctx - 1, n_ctx)

    barrier = pltpu.get_barrier_semaphore()

    def greet(d, carry):
        pl.semaphore_signal(
            barrier, inc=1, device_id=(lax.rem(z + d, n_ctx), hd), device_id_type=MESH
        )
        return carry

    lax.fori_loop(1, n_ctx, greet, 0)
    for d in range(1, 4):
        pl.semaphore_signal(
            barrier, inc=1, device_id=(z, base + lax.rem(place + d, 4)), device_id_type=MESH
        )

    for i in range(4):
        kvbuf[z, i] = kv_ref[0, i * 128 : (i + 1) * 128, :]
        kvbuf[z, 4 + i] = kv_ref[1, i * 128 : (i + 1) * 128, :].T
    for h in range(2):
        for i in range(4):
            qt[:, h * 512 + i * 128 : h * 512 + (i + 1) * 128] = q_ref[
                i * 128 : (i + 1) * 128, h * 128 : (h + 1) * 128
            ].T

    step = step_ref[...]
    raw = jnp.concatenate([step[:, k * SPAN : (k + 1) * SPAN] for k in range(4)], axis=0)
    row16 = lax.broadcasted_iota(jnp.int32, (16, SPAN), 0)
    rate = jnp.zeros((16, SPAN), jnp.float32)
    for h in range(4):
        rate = jnp.where(lax.rem(row16, 4) == h, decay_ref[h], rate)
    dt = softplus(raw)
    ell = -jnp.exp(rate) * dt
    upper = (
        lax.broadcasted_iota(jnp.int32, (SPAN, SPAN), 0)
        <= lax.broadcasted_iota(jnp.int32, (SPAN, SPAN), 1)
    ).astype(jnp.float32)
    cumul = dot(ell, upper, precision=HIGH)
    ends = cumul[:, SPAN - 1 : SPAN]
    tail = jnp.exp(ends - cumul) * dt
    offsets = [jnp.zeros((4, 1), jnp.float32)]
    for k in range(4):
        offsets.append(offsets[-1] + ends[k * 4 : (k + 1) * 4])
    from_start = cumul + jnp.concatenate(offsets[:4], axis=0)
    lane2 = lax.broadcasted_iota(jnp.int32, (2, 128), 1)
    total_rows = []
    for i in range(2):
        a = jnp.broadcast_to(offsets[4][2 * i : 2 * i + 1], (1, 128))
        b = jnp.broadcast_to(offsets[4][2 * i + 1 : 2 * i + 2], (1, 128))
        total_rows.append(jnp.where(lane2[0:1] < 64, a, b))
    total_buf[z] = jnp.concatenate(total_rows, axis=0)

    pl.semaphore_wait(barrier, n_ctx - 1 + 3)

    def up_copy(s, c):
        block = lax.rem(z - s + n_ctx, n_ctx)
        return pltpu.make_async_remote_copy(
            src_ref=kvbuf.at[block, core * 4 + c],
            dst_ref=kvbuf.at[block, core * 4 + c],
            send_sem=up_send.at[s * CHUNKS + c],
            recv_sem=up_recv.at[s * CHUNKS + c],
            device_id=(above, hd),
            device_id_type=MESH,
        )

    def down_copy(s, c):
        block = lax.rem(z + s, n_ctx)
        return pltpu.make_async_remote_copy(
            src_ref=kvbuf.at[block, core * 4 + c],
            dst_ref=kvbuf.at[block, core * 4 + c],
            send_sem=dn_send.at[s * CHUNKS + c],
            recv_sem=dn_recv.at[s * CHUNKS + c],
            device_id=(below, hd),
            device_id_type=MESH,
        )

    def up_arrival(s, c):
        block = lax.rem(z - s + n_ctx, n_ctx)
        return pltpu.make_async_remote_copy(
            src_ref=kvbuf.at[block, core * 4 + c],
            dst_ref=kvbuf.at[block, core * 4 + c],
            send_sem=up_send.at[(s - 1) * CHUNKS + c],
            recv_sem=up_recv.at[(s - 1) * CHUNKS + c],
            device_id=(above, hd),
            device_id_type=MESH,
        )

    def down_arrival(s, c):
        block = lax.rem(z + s, n_ctx)
        return pltpu.make_async_remote_copy(
            src_ref=kvbuf.at[block, core * 4 + c],
            dst_ref=kvbuf.at[block, core * 4 + c],
            send_sem=dn_send.at[(s - 1) * CHUNKS + c],
            recv_sem=dn_recv.at[(s - 1) * CHUNKS + c],
            device_id=(below, hd),
            device_id_type=MESH,
        )

    def sib_copy(block, part, send, recv, i):
        return pltpu.make_async_remote_copy(
            src_ref=kvbuf.at[block, part],
            dst_ref=kvbuf.at[block, part],
            send_sem=send.at[i],
            recv_sem=recv.at[i],
            device_id=(z, sib),
            device_id_type=MESH,
        )

    def up_block(s):
        return lax.rem(z - s + n_ctx, n_ctx)

    def down_block(s):
        return lax.rem(z + s, n_ctx)

    def travels_down(s):
        return lax.rem(z + s, n_ctx) <= n_ctx - 2 - UP

    def down_useful(s):
        return jnp.logical_and(z + s >= n_ctx, travels_down(s))

    for c in range(CHUNKS):

        @pl.when(z < n_ctx - 1)
        def _():
            up_copy(0, c).start()

        @pl.when(travels_down(0))
        def _():
            down_copy(0, c).start()

    def total_copy(d):
        return pltpu.make_async_remote_copy(
            src_ref=total_buf.at[z],
            dst_ref=total_buf.at[z],
            send_sem=d_send.at[d],
            recv_sem=d_recv.at[z],
            device_id=(lax.rem(z + d, n_ctx), hd),
            device_id_type=MESH,
        )

    def total_arrival(d):
        other = lax.rem(z + d, n_ctx)
        return pltpu.make_async_remote_copy(
            src_ref=total_buf.at[other],
            dst_ref=total_buf.at[other],
            send_sem=d_send.at[d],
            recv_sem=d_recv.at[other],
            device_id=(other, hd),
            device_id_type=MESH,
        )

    def state_copy(d):
        other = lax.rem(z + d, n_ctx)
        return pltpu.make_async_remote_copy(
            src_ref=sbuf.at[other],
            dst_ref=srecv.at[z],
            send_sem=s_send.at[d],
            recv_sem=s_recv.at[z],
            device_id=(other, hd),
            device_id_type=MESH,
        )

    def state_arrival(d):
        other = lax.rem(z + d, n_ctx)
        return pltpu.make_async_remote_copy(
            src_ref=sbuf.at[other],
            dst_ref=srecv.at[other],
            send_sem=s_send.at[d],
            recv_sem=s_recv.at[other],
            device_id=(other, hd),
            device_id_type=MESH,
        )

    def entering_copy(d):
        other = lax.rem(z + d, n_ctx)
        return pltpu.make_async_remote_copy(
            src_ref=ebuf.at[other],
            dst_ref=erecv.at[z],
            send_sem=e_send.at[d],
            recv_sem=e_recv.at[z],
            device_id=(other, hd),
            device_id_type=MESH,
        )

    def entering_arrival(d):
        other = lax.rem(z + d, n_ctx)
        return pltpu.make_async_remote_copy(
            src_ref=ebuf.at[other],
            dst_ref=erecv.at[other],
            send_sem=e_send.at[d],
            recv_sem=e_recv.at[other],
            device_id=(other, hd),
            device_id_type=MESH,
        )

    def each(first, last, action, cond=None):
        def turn(d, carry):
            if cond is None:
                action(d)
            else:

                @pl.when(cond(d))
                def _():
                    action(d)

            return carry

        lax.fori_loop(first, last, turn, 0)

    def other_of(d):
        return lax.rem(z + d, n_ctx)

    last = n_ctx - 1

    @pl.when(z < last)
    def _():
        each(1, n_ctx, lambda d: total_copy(d).start())

    row_r = lax.broadcasted_iota(jnp.int32, (16, 256), 0)
    head_l = lax.broadcasted_iota(jnp.int32, (16, 256), 1) // 64
    tail_t, cumul_t, start_t = tail.T, cumul.T, from_start.T
    running = None
    run_list = []
    for k in range(4):
        rows = slice(k * SPAN, (k + 1) * SPAN)
        pick = (row_r == k * 4 + head_l).astype(jnp.float32)
        tail_x = dot(tail_t, pick, precision=HIGH)
        decay_t[rows, :] = jnp.exp(dot(start_t, pick, precision=HIGH))
        loads = (x_ref[rows, :].astype(jnp.float32) * tail_x).astype(jnp.bfloat16)
        fresh = dot(maps_ref[0, rows, :].T, loads)
        end_lane = jnp.sum(jnp.broadcast_to(ends, (16, 256)) * pick, axis=0, keepdims=True)
        running = fresh if k == 0 else jnp.exp(end_lane) * running + fresh
        run_list.append(running)
    for i in range(n_ctx):
        half, r = i // 8, i % 8
        sbuf[i] = running[r * 16 : (r + 1) * 16, half * 128 : (half + 1) * 128].astype(
            jnp.bfloat16
        )

    @pl.when(z < last)
    def _():
        each(1, n_ctx, lambda d: state_copy(d).start())

    lane_w = lax.broadcasted_iota(jnp.int32, (SPAN, SPAN), 1)
    below_diag = lax.broadcasted_iota(jnp.int32, (SPAN, SPAN), 0) >= lane_w
    lane_p = lax.broadcasted_iota(jnp.int32, (1, 256), 1) // 64
    skip = jnp.zeros((1, 256), jnp.float32)
    for h in range(4):
        skip = jnp.where(lane_p == h, skip_ref[h], skip)
    left = lane_w < 64
    for k in range(4):
        rows = slice(k * SPAN, (k + 1) * SPAN)
        b_mat, c_mat = maps_ref[0, rows, :], maps_ref[1, rows, :]
        scores = dot_t(c_mat, b_mat)
        for pair in range(2):
            lanes = slice(pair * 128, (pair + 1) * 128)
            x_pair = x_ref[rows, lanes]
            weights = []
            for h in (2 * pair, 2 * pair + 1):
                r = k * 4 + h
                spread = cumul_t[:, r : r + 1] - cumul[r : r + 1, :]
                grown = jnp.exp(jnp.where(below_diag, spread, NEG_FILL))
                weights.append((scores * grown * dt[r : r + 1, :]).astype(jnp.bfloat16))
            zero = jnp.zeros_like(x_pair)
            x_two = jnp.concatenate(
                [jnp.where(left, x_pair, zero), jnp.where(left, zero, x_pair)], axis=0
            )
            inside = dot(jnp.concatenate(weights, axis=1), x_two)
            total = inside + skip[:, lanes] * x_pair.astype(jnp.float32)
            mixed[rows, lanes] = total
        if k > 0:
            pick = (row_r == k * 4 + head_l).astype(jnp.float32)
            grown_in = jnp.exp(dot(cumul_t, pick, precision=HIGH))
            mixed[rows, :] += dot(c_mat, run_list[k - 1].astype(jnp.bfloat16)) * grown_in

    coef = math.log2(math.e) / math.sqrt(128.0)

    def diagonal(t):
        lanes = slice(t * 128, (t + 1) * 128)
        tile = t % 4
        count = (tile + 1) * 128
        k_mat = kvbuf[z, 0 : tile + 1].reshape(count, 128)
        s = dot(k_mat, qt[:, lanes])
        key = lax.broadcasted_iota(jnp.int32, (count, 128), 0)
        query = lax.broadcasted_iota(jnp.int32, (count, 128), 1) + tile * 128
        s = jnp.where(key <= query, s, NEG_FILL)
        m = jnp.max(s, axis=0, keepdims=True)
        p = jnp.exp2((s - m) * coef)
        m_run[:, lanes] = m
        l_run[:, lanes] = jnp.sum(p, axis=0, keepdims=True)
        v_mat = jnp.concatenate([kvbuf[z, 4 + i] for i in range(tile + 1)], axis=1)
        acc[:, lanes] = dot(v_mat, p.astype(jnp.bfloat16))

    def attend(block, t):
        lanes = slice(t * 128, (t + 1) * 128)
        s = dot(kvbuf[block, 0:4].reshape(512, 128), qt[:, lanes])
        before = m_run[:, lanes]
        m = jnp.maximum(before, jnp.max(s, axis=0, keepdims=True))
        p = jnp.exp2((s - m) * coef)
        scale = jnp.exp2((before - m) * coef)
        m_run[:, lanes] = m
        l_run[:, lanes] = l_run[:, lanes] * scale + jnp.sum(p, axis=0, keepdims=True)
        v_mat = jnp.concatenate([kvbuf[block, 4 + i] for i in range(4)], axis=1)
        acc[:, lanes] = acc[:, lanes] * scale + dot(v_mat, p.astype(jnp.bfloat16))

    for t in range(8):
        diagonal(t)

    def prefix():
        each(
            1,
            n_ctx,
            lambda d: (total_arrival(d).wait_recv(), state_arrival(d).wait_recv()),
            lambda d: other_of(d) < last,
        )
        srecv[z] = sbuf[z]
        half = z // 8
        entering = jnp.zeros((16, 128), jnp.float32)
        for k in range(n_ctx):
            ebuf[k] = entering.astype(jnp.bfloat16)
            if k < last:
                entering = (
                    jnp.exp(total_buf[k, pl.ds(half, 1), :]) * entering
                    + srecv[k].astype(jnp.float32)
                )
        erecv[z] = ebuf[z]
        each(1, n_ctx, lambda d: entering_copy(d).start(), lambda d: other_of(d) > 0)

    def finish_mixed():
        @pl.when(z > 0)
        def _():
            each(1, n_ctx, lambda d: entering_arrival(d).wait_recv())
            e_mat = [erecv[i * 8 : (i + 1) * 8].reshape(128, 128) for i in range(2)]
            for k in range(4):
                rows = slice(k * SPAN, (k + 1) * SPAN)
                for i in range(2):
                    lanes = slice(i * 128, (i + 1) * 128)
                    mixed[rows, lanes] += dot(maps_ref[1, rows, :], e_mat[i]) * decay_t[rows, lanes]

        ones = jnp.ones((8, 256), jnp.bfloat16)
        for k in range(4):
            rows = slice(k * SPAN, (k + 1) * SPAN)
            value = mixed[rows, :] * silu(gate_ref[rows, :].astype(jnp.float32))
            gated[rows, :] = value
            squares = (value * value).astype(jnp.bfloat16)
            sq_buf[place, :, k * SPAN : (k + 1) * SPAN] = dot_t(ones, squares)
        for d in range(1, 4):
            square_copy(d).start()

    def square_copy(d):
        return pltpu.make_async_remote_copy(
            src_ref=sq_buf.at[place],
            dst_ref=sq_buf.at[place],
            send_sem=q_send.at[d],
            recv_sem=q_recv.at[place],
            device_id=(z, base + lax.rem(place + d, 4)),
            device_id_type=MESH,
        )

    def square_arrival(d):
        other = lax.rem(place + d, 4)
        return pltpu.make_async_remote_copy(
            src_ref=sq_buf.at[other],
            dst_ref=sq_buf.at[other],
            send_sem=q_send.at[d],
            recv_sem=q_recv.at[other],
            device_id=(z, base + other),
            device_id_type=MESH,
        )

    def finish_norm():
        for d in range(1, 4):
            square_arrival(d).wait_recv()
        total = sq_buf[0] + sq_buf[1] + sq_buf[2] + sq_buf[3]
        inv = lax.rsqrt(total * (1.0 / 1024.0) + EPSILON)
        row8 = lax.broadcasted_iota(jnp.int32, (8, 256), 0)
        gain = jnp.broadcast_to(gain_ref[...].reshape(1, 256), (8, 256))
        gain = jnp.where(row8 == 0, gain, 0.0)
        for k in range(4):
            rows = slice(k * SPAN, (k + 1) * SPAN)
            factor = dot(inv[:, k * SPAN : (k + 1) * SPAN].T, gain, precision=HIGH)
            mamba_ref[rows, :] = (gated[rows, :] * factor).astype(jnp.bfloat16)

    def ring(s, carry):
        for c in range(CHUNKS):

            @pl.when(z >= s)
            def _():
                up_arrival(s, c).wait_recv()

                @pl.when(jnp.logical_and(z < last, s < UP))
                def _():
                    up_copy(s, c).start()

                sib_copy(up_block(s), core * 4 + c, sib_send, sib_recv, s * CHUNKS + c).start()

            @pl.when(jnp.logical_and(s <= DOWN, travels_down(s)))
            def _():
                down_arrival(s, c).wait_recv()

                @pl.when(s < DOWN)
                def _():
                    down_copy(s, c).start()

                @pl.when(z + s >= n_ctx)
                def _():
                    sib_copy(
                        down_block(s), core * 4 + c, sibd_send, sibd_recv, s * CHUNKS + c
                    ).start()

            if c == 0:
                sib_wait(s - 1)
            attend_two(s - 1, c)

        @pl.when(s == M4_STEP)
        def _():
            prefix()

        @pl.when(s == M5_STEP)
        def _():
            finish_mixed()

        return carry

    def sib_wait(s):
        @pl.when(jnp.logical_and(s >= 1, z >= s))
        def _():
            for c in range(CHUNKS):
                sib_copy(
                    up_block(s), (1 - core) * 4 + c, sib_send, sib_recv, s * CHUNKS + c
                ).wait_recv()

        @pl.when(jnp.logical_and(jnp.logical_and(s >= 1, s <= DOWN), down_useful(s)))
        def _():
            for c in range(CHUNKS):
                sib_copy(
                    down_block(s), (1 - core) * 4 + c, sibd_send, sibd_recv, s * CHUNKS + c
                ).wait_recv()

    def attend_two(s, c):
        @pl.when(jnp.logical_and(s >= 1, z >= s))
        def _():
            attend(up_block(s), 2 * c)
            attend(up_block(s), 2 * c + 1)

        @pl.when(jnp.logical_and(jnp.logical_and(s >= 1, s <= DOWN), down_useful(s)))
        def _():
            attend(down_block(s), 2 * c)
            attend(down_block(s), 2 * c + 1)

    lax.fori_loop(1, UP + 1, ring, 0)
    sib_wait(UP)

    @pl.when(z >= UP)
    def _():
        for t in range(8):
            attend(up_block(UP), t)

    finish_norm()
    for h in range(2):
        for i in range(4):
            lanes = slice(h * 512 + i * 128, h * 512 + (i + 1) * 128)
            result = acc[:, lanes] / l_run[:, lanes]
            attn_ref[i * 128 : (i + 1) * 128, h * 128 : (h + 1) * 128] = result.T.astype(
                jnp.bfloat16
            )

    def sent(s, carry):
        for c in range(CHUNKS):

            @pl.when(jnp.logical_and(z >= s, z < last))
            def _():
                up_copy(s, c).wait_send()

            @pl.when(jnp.logical_and(s < DOWN, travels_down(s)))
            def _():
                down_copy(s, c).wait_send()

        return carry

    def sent_sib(s, carry):
        for c in range(CHUNKS):

            @pl.when(z >= s)
            def _():
                sib_copy(up_block(s), core * 4 + c, sib_send, sib_recv, s * CHUNKS + c).wait_send()

            @pl.when(jnp.logical_and(s <= DOWN, down_useful(s)))
            def _():
                sib_copy(
                    down_block(s), core * 4 + c, sibd_send, sibd_recv, s * CHUNKS + c
                ).wait_send()

        return carry

    lax.fori_loop(0, UP, sent, 0)
    lax.fori_loop(1, UP + 1, sent_sib, 0)

    @pl.when(z < last)
    def _():
        each(1, n_ctx, lambda d: (total_copy(d).wait_send(), state_copy(d).wait_send()))

    each(1, n_ctx, lambda d: entering_copy(d).wait_send(), lambda d: other_of(d) > 0)
    for d in range(1, 4):
        square_copy(d).wait_send()


def body(
    n_ctx,
    mixer_input,
    gate_input,
    step_raw,
    decay_log,
    skip_weight,
    state_maps,
    norm_gain,
    queries,
    keys_values,
):
    group = lax.axis_index("head") // 4
    maps = lax.dynamic_index_in_dim(state_maps, group, axis=2, keepdims=False)
    pairs = lax.dynamic_index_in_dim(keys_values, group, axis=2, keepdims=False)
    maps = maps.transpose(1, 0, 2)
    pairs = pairs.transpose(1, 0, 2)
    vmem = pl.BlockSpec(memory_space=pltpu.VMEM)
    smem = pl.BlockSpec(memory_space=pltpu.SMEM)
    dma = pltpu.SemaphoreType.DMA
    rows = mixer_input.shape[0]
    return pl.pallas_call(
        functools.partial(kernel, n_ctx),
        out_shape=(
            jax.ShapeDtypeStruct((rows, 256), jnp.bfloat16),
            jax.ShapeDtypeStruct((rows, 256), jnp.bfloat16),
        ),
        in_specs=[smem, smem] + [vmem] * 7,
        out_specs=(vmem, vmem),
        scratch_shapes=[
            pltpu.VMEM((n_ctx, 8, 128, 128), jnp.bfloat16),
            pltpu.VMEM((128, 1024), jnp.bfloat16),
            pltpu.VMEM((1, 1024), jnp.float32),
            pltpu.VMEM((1, 1024), jnp.float32),
            pltpu.VMEM((128, 1024), jnp.float32),
            pltpu.VMEM((512, 256), jnp.float32),
            pltpu.VMEM((512, 256), jnp.float32),
            pltpu.VMEM((512, 256), jnp.float32),
            pltpu.VMEM((n_ctx, 2, 128), jnp.float32),
            pltpu.VMEM((n_ctx, 16, 128), jnp.bfloat16),
            pltpu.VMEM((n_ctx, 16, 128), jnp.bfloat16),
            pltpu.VMEM((n_ctx, 16, 128), jnp.bfloat16),
            pltpu.VMEM((n_ctx, 16, 128), jnp.bfloat16),
            pltpu.VMEM((4, 8, 512), jnp.float32),
            dma((UP * CHUNKS,)),
            dma((UP * CHUNKS,)),
            dma((DOWN * CHUNKS,)),
            dma((DOWN * CHUNKS,)),
            dma(((UP + 1) * CHUNKS,)),
            dma(((UP + 1) * CHUNKS,)),
            dma(((DOWN + 1) * CHUNKS,)),
            dma(((DOWN + 1) * CHUNKS,)),
            dma((n_ctx,)),
            dma((n_ctx,)),
            dma((n_ctx,)),
            dma((n_ctx,)),
            dma((n_ctx,)),
            dma((n_ctx,)),
            dma((4,)),
            dma((4,)),
        ],
        compiler_params=pltpu.CompilerParams(
            collective_id=0, has_side_effects=True, vmem_limit_bytes=40 * 2**20
        ),
    )(
        decay_log,
        skip_weight,
        step_raw.T,
        mixer_input,
        gate_input,
        maps,
        norm_gain,
        queries,
        pairs,
    )


def solution(mesh):
    in_specs = (
        P("ctx", "head"),
        P("ctx", "head"),
        P("ctx", "head"),
        P("head"),
        P("head"),
        P("ctx", None, None, None),
        P("head"),
        P("ctx", "head"),
        P("ctx", None, None, None),
    )
    return jax.shard_map(
        functools.partial(body, mesh.shape["ctx"]),
        mesh=mesh,
        in_specs=in_specs,
        out_specs=(P("ctx", "head"), P("ctx", "head")),
        check_vma=False,
    )
```

time: 368 us -> 59.4 us (0.16)
  the two profiles are of different devices: /device:TPU:480 before, /device:TPU:485 now
where the time goes in v1:
time: 59.4 us; the launch traced here: 59.2 us
  Pallas kernels  53.5 us (90%)
  local copies, waits for them, and re-layouts  4.95 us (8%)
  between operations  0.79 us (1%)
    pallas_call x1, Pallas kernels, body(): pl.pallas_call(functools.partial(kernel, n_ctx), out_shape=(jax.ShapeDtyp...  53.5 us
    dynamic_slice x2, local copies, waits for them, and re-layouts, body(): pairs = lax.dynamic_index_in_dim(keys_values, group, axis=2, keepdims=False)  3.46 us
    unnamed x16, local copies, waits for them, and re-layouts  1.44 us

profile of v1, /device:TPU:485, one launch (start us, length us, event | category | flops | bytes accessed | tf_op | source)
XLA Modules:
  0.0 59.2 jit_solution(10953022965671213679)
XLA Ops:
  0.6 0.0 copy-start.2
  0.6 0.0 copy-start.4
  0.7 0.0 copy-start.6
  0.7 0.0 copy-start.5
  0.7 0.0 copy-start.3
  0.7 0.0 copy-start.1
  0.7 0.0 copy-start
  0.7 3.4 %constant_dynamic-slice_fusion = (bf16[512,2,1,128]{3,2,1,0:T(2,128)(2,1)S(1)}, bf16[512,2,1,128]{3,2,1,0:T(2,128)(2,1)S(1)}) fusion(bf16[512,2,8,128]{3,2,1,0:T(8,128)(2,1)} %param.17, s32[]{:T(128)S(6)} %select_n.11, bf16[512,2,8,128]{3,2,1,0:T(8,128)(2,1)} %param.14), kind=kLoop, calls=%fused_computation.2 | loop fusion | bytes 1048580 | tf_op jit(solution)/shard_map/jit(dynamic_index_in_dim)/dynamic_slice | solution.py:615
  4.2 0.0 copy-done.2
  4.3 0.0 copy-done.4
  4.3 0.0 copy-done.6
  4.3 0.0 copy-done.5
  4.3 0.0 copy-done.3
  4.3 0.0 copy-done.1
  4.3 0.0 copy-done
  4.3 53.5 %shard_map.104 = (bf16[512,256]{1,0:T(8,128)(2,1)S(1)}, bf16[512,256]{1,0:T(8,128)(2,1)S(1)}) custom-call(f32[4]{0:T(128)S(1)} %copy-done.5, f32[4]{0:T(128)S(1)} %copy-done.6, f32[4,512]{1,0:T(4,128)S(1)} %bitcast.13, bf16[512,256]{1,0:T(8,128)(2,1)S(1)} %copy-done, bf16[512,256]{1,0:T(8,128)(2,1)S(1)} %copy-done.1, bf16[2,512,128]{2,1,0:T(8,128)(2,1)S(1)} %bitcast.12, ...), custom_call_target="tpu_custom_call" | custom-call | tf_op jit(solution)/shard_map/pallas_call | solution.py:622
  57.8 0.7 %copy.19 = bf16[512,256]{1,0:T(8,128)(2,1)} copy(bf16[512,256]{1,0:T(8,128)(2,1)S(1)} %get-tuple-element.6) | data formatting | bytes 524288
  58.5 0.7 %copy.20 = bf16[512,256]{1,0:T(8,128)(2,1)} copy(bf16[512,256]{1,0:T(8,128)(2,1)S(1)} %get-tuple-element.7) | data formatting | bytes 524288
  (2 shorter events, 0.1 us)
Async XLA Ops:
  0.6 3.6 %copy-start.2 = (bf16[512,256]{1,0:T(8,128)(2,1)S(1)}, bf16[512,256]{1,0:T(8,128)(2,1)}, u32[]{:S(2)}) copy-start(bf16[512,256]{1,0:T(8,128)(2,1)} %q_ref.1) | copy-start | bytes 786436
  0.6 3.6 %copy-start.4 = (f32[256]{0:T(256)S(1)}, f32[256]{0:T(256)}, u32[]{:S(2)}) copy-start(f32[256]{0:T(256)} %gain_ref.1) | copy-start | bytes 3076
  0.7 3.6 %copy-start.6 = (f32[4]{0:T(128)S(1)}, f32[4]{0:T(128)}, u32[]{:S(2)}) copy-start(f32[4]{0:T(128)} %skip_ref.1) | copy-start | bytes 52
  0.7 3.6 %copy-start.5 = (f32[4]{0:T(128)S(1)}, f32[4]{0:T(128)}, u32[]{:S(2)}) copy-start(f32[4]{0:T(128)} %decay_ref.1) | copy-start | bytes 52
  0.7 3.6 %copy-start.3 = (f32[512,4]{0,1:T(4,128)S(1)}, f32[512,4]{0,1:T(4,128)}, u32[]{:S(2)}) copy-start(f32[512,4]{0,1:T(4,128)} %param.11) | copy-start | bytes 24580
  0.7 3.6 %copy-start.1 = (bf16[512,256]{1,0:T(8,128)(2,1)S(1)}, bf16[512,256]{1,0:T(8,128)(2,1)}, u32[]{:S(2)}) copy-start(bf16[512,256]{1,0:T(8,128)(2,1)} %gate_ref.1) | copy-start | bytes 786436
  0.7 3.6 %copy-start = (bf16[512,256]{1,0:T(8,128)(2,1)S(1)}, bf16[512,256]{1,0:T(8,128)(2,1)}, u32[]{:S(2)}) copy-start(bf16[512,256]{1,0:T(8,128)(2,1)} %x_ref.1) | copy-start | bytes 786436

commit v2 on v1

--- a/solution.py
+++ b/solution.py
@@ -15,7 +15,9 @@
 SPAN = 128
 CHUNKS = 4
 UP = 8
-DOWN = 7
+HALF = CHUNKS // 2
+NEAR = 2
+STATE_STEP = 1
 M4_STEP = 4
 M5_STEP = 7
 
@@ -32,6 +34,14 @@
 
 def dot(a, b, **kw):
     return jnp.dot(a, b, preferred_element_type=jnp.float32, **kw)
+
+
+def parts_of(v):
+    high = v.astype(jnp.bfloat16)
+    rest = v - high.astype(jnp.float32)
+    middle = rest.astype(jnp.bfloat16)
+    low = (rest - middle.astype(jnp.float32)).astype(jnp.bfloat16)
+    return high, middle, low
 
 
 def dot_t(a, b, **kw):
@@ -45,14 +55,23 @@
     decay_ref,
     skip_ref,
     step_ref,
+    gain_ref,
+    x_hbm,
+    gate_hbm,
+    maps_hbm,
+    q_hbm,
+    kv_hbm,
+    mamba_ref,
+    attn_ref,
     x_ref,
     gate_ref,
+    q_ref,
+    maps_raw,
+    kv_raw,
+    wide,
     maps_ref,
-    gain_ref,
-    q_ref,
-    kv_ref,
-    mamba_ref,
-    attn_ref,
+    in_sem,
+    far_sem,
     kvbuf,
     qt,
     m_run,
@@ -94,27 +113,41 @@
     below = lax.rem(z + n_ctx - 1, n_ctx)
 
     barrier = pltpu.get_barrier_semaphore()
-
-    def greet(d, carry):
-        pl.semaphore_signal(
-            barrier, inc=1, device_id=(lax.rem(z + d, n_ctx), hd), device_id_type=MESH
-        )
-        return carry
-
-    lax.fori_loop(1, n_ctx, greet, 0)
+    for d in range(NEAR, 0, -1):
+        for other in (lax.rem(z + d, n_ctx), lax.rem(z + n_ctx - d, n_ctx)):
+            pl.semaphore_signal(barrier, inc=1, device_id=(other, hd), device_id_type=MESH)
     for d in range(1, 4):
         pl.semaphore_signal(
             barrier, inc=1, device_id=(z, base + lax.rem(place + d, 4)), device_id_type=MESH
         )
 
+    fetches = []
+    for src, dst in ((kv_hbm, kv_raw), (maps_hbm, maps_raw)):
+        for rows in (pl.ds(0, 4096), pl.ds(4096, 4096)):
+            fetches.append((src.at[rows], dst.at[rows]))
+    fetches += [(q_hbm, q_ref), (x_hbm, x_ref), (gate_hbm, gate_ref)]
+    fetches = [
+        pltpu.make_async_copy(src, dst, in_sem.at[i]) for i, (src, dst) in enumerate(fetches)
+    ]
+    for fetch in fetches:
+        fetch.start()
+
+    def pick_group(raw, waits):
+        for i, fetch in enumerate(waits):
+            fetch.wait()
+
+            def widen(k, carry):
+                rows = pl.ds(pl.multiple_of(i * 4096 + k * 512, 512), 512)
+                wide[rows, :] = raw[rows, :].astype(jnp.float32)
+                return carry
+
+            lax.fori_loop(0, 8, widen, 0)
+        return [wide[pl.ds(8 * i + hd // 4, 512, stride=16), :] for i in range(2)]
+
+    keys, values = pick_group(kv_raw, fetches[0:2])
     for i in range(4):
-        kvbuf[z, i] = kv_ref[0, i * 128 : (i + 1) * 128, :]
-        kvbuf[z, 4 + i] = kv_ref[1, i * 128 : (i + 1) * 128, :].T
-    for h in range(2):
-        for i in range(4):
-            qt[:, h * 512 + i * 128 : h * 512 + (i + 1) * 128] = q_ref[
-                i * 128 : (i + 1) * 128, h * 128 : (h + 1) * 128
-            ].T
+        kvbuf[z, i] = keys[i * 128 : (i + 1) * 128, :].astype(jnp.bfloat16)
+        kvbuf[z, 4 + i] = values[i * 128 : (i + 1) * 128, :].T.astype(jnp.bfloat16)
 
     step = step_ref[...]
     raw = jnp.concatenate([step[:, k * SPAN : (k + 1) * SPAN] for k in range(4)], axis=0)
@@ -143,8 +176,6 @@
         total_rows.append(jnp.where(lane2[0:1] < 64, a, b))
     total_buf[z] = jnp.concatenate(total_rows, axis=0)
 
-    pl.semaphore_wait(barrier, n_ctx - 1 + 3)
-
     def up_copy(s, c):
         block = lax.rem(z - s + n_ctx, n_ctx)
         return pltpu.make_async_remote_copy(
@@ -205,21 +236,21 @@
     def down_block(s):
         return lax.rem(z + s, n_ctx)
 
-    def travels_down(s):
-        return lax.rem(z + s, n_ctx) <= n_ctx - 2 - UP
-
-    def down_useful(s):
-        return jnp.logical_and(z + s >= n_ctx, travels_down(s))
-
-    for c in range(CHUNKS):
-
-        @pl.when(z < n_ctx - 1)
-        def _():
-            up_copy(0, c).start()
-
-        @pl.when(travels_down(0))
-        def _():
-            down_copy(0, c).start()
+    def up_hops(c):
+        return UP if c < HALF else UP - 1
+
+    def down_hops(c):
+        return UP - 1 if c < HALF else UP
+
+    def came_up(s, c):
+        return jnp.logical_and(z >= s, s <= up_hops(c))
+
+    def travels_down(s, c):
+        block = lax.rem(z + s, n_ctx)
+        return jnp.logical_and(block < down_hops(c), s <= down_hops(c))
+
+    def down_useful(s, c):
+        return jnp.logical_and(z + s >= n_ctx, travels_down(s, c))
 
     def total_copy(d):
         return pltpu.make_async_remote_copy(
@@ -305,20 +336,23 @@
 
     last = n_ctx - 1
 
-    @pl.when(z < last)
-    def _():
-        each(1, n_ctx, lambda d: total_copy(d).start())
-
+    b_all, c_all = pick_group(maps_raw, fetches[2:4])
+    maps_ref[0] = b_all.astype(jnp.bfloat16)
+    maps_ref[1] = c_all.astype(jnp.bfloat16)
+    fetches[5].wait()
     row_r = lax.broadcasted_iota(jnp.int32, (16, 256), 0)
     head_l = lax.broadcasted_iota(jnp.int32, (16, 256), 1) // 64
-    tail_t, cumul_t, start_t = tail.T, cumul.T, from_start.T
+    tail_t, start_t = (jnp.concatenate(parts_of(v.T), axis=1) for v in (tail, from_start))
+    cumul_t = cumul.T
+    cumul_3 = jnp.concatenate(parts_of(cumul_t), axis=1)
     running = None
     run_list = []
     for k in range(4):
         rows = slice(k * SPAN, (k + 1) * SPAN)
         pick = (row_r == k * 4 + head_l).astype(jnp.float32)
-        tail_x = dot(tail_t, pick, precision=HIGH)
-        decay_t[rows, :] = jnp.exp(dot(start_t, pick, precision=HIGH))
+        pick_3 = jnp.concatenate([pick.astype(jnp.bfloat16)] * 3, axis=0)
+        tail_x = dot(tail_t, pick_3)
+        decay_t[rows, :] = jnp.exp(dot(start_t, pick_3))
         loads = (x_ref[rows, :].astype(jnp.float32) * tail_x).astype(jnp.bfloat16)
         fresh = dot(maps_ref[0, rows, :].T, loads)
         end_lane = jnp.sum(jnp.broadcast_to(ends, (16, 256)) * pick, axis=0, keepdims=True)
@@ -330,9 +364,37 @@
             jnp.bfloat16
         )
 
-    @pl.when(z < last)
-    def _():
-        each(1, n_ctx, lambda d: state_copy(d).start())
+    fetches[4].wait()
+    for h in range(2):
+        for i in range(4):
+            qt[:, h * 512 + i * 128 : h * 512 + (i + 1) * 128] = q_ref[
+                i * 128 : (i + 1) * 128, h * 128 : (h + 1) * 128
+            ].T
+
+    pl.semaphore_wait(barrier, 2 * NEAR + 3)
+    for c in range(CHUNKS):
+
+        @pl.when(z < n_ctx - 1)
+        def _():
+            up_copy(0, c).start()
+
+        @pl.when(travels_down(0, c))
+        def _():
+            down_copy(0, c).start()
+
+    def tell(i):
+        d = NEAR * 2**i
+        for other in (lax.rem(z + d, n_ctx), lax.rem(z + n_ctx - d, n_ctx)):
+            pl.semaphore_signal(far_sem.at[i], inc=1, device_id=(other, hd), device_id_type=MESH)
+
+    tell(0)
+
+    def send_states():
+        pl.semaphore_wait(far_sem.at[1], 2)
+
+        @pl.when(z < last)
+        def _():
+            each(1, n_ctx, lambda d: (total_copy(d).start(), state_copy(d).start()))
 
     lane_w = lax.broadcasted_iota(jnp.int32, (SPAN, SPAN), 1)
     below_diag = lax.broadcasted_iota(jnp.int32, (SPAN, SPAN), 0) >= lane_w
@@ -362,8 +424,8 @@
             total = inside + skip[:, lanes] * x_pair.astype(jnp.float32)
             mixed[rows, lanes] = total
         if k > 0:
-            pick = (row_r == k * 4 + head_l).astype(jnp.float32)
-            grown_in = jnp.exp(dot(cumul_t, pick, precision=HIGH))
+            pick = (row_r == k * 4 + head_l).astype(jnp.bfloat16)
+            grown_in = jnp.exp(dot(cumul_3, jnp.concatenate([pick] * 3, axis=0)))
             mixed[rows, :] += dot(c_mat, run_list[k - 1].astype(jnp.bfloat16)) * grown_in
 
     coef = math.log2(math.e) / math.sqrt(128.0)
@@ -384,17 +446,27 @@
         v_mat = jnp.concatenate([kvbuf[z, 4 + i] for i in range(tile + 1)], axis=1)
         acc[:, lanes] = dot(v_mat, p.astype(jnp.bfloat16))
 
-    def attend(block, t):
-        lanes = slice(t * 128, (t + 1) * 128)
-        s = dot(kvbuf[block, 0:4].reshape(512, 128), qt[:, lanes])
+    ones = jnp.ones((16, 256), jnp.bfloat16)
+
+    def attend(blocks, t):
+        lanes = slice(t * 256, (t + 1) * 256)
+        queries = qt[:, lanes]
+        parts = [(b, i) for b in blocks for i in range(2)]
+        scores = [dot(kvbuf[b, 2 * i : 2 * i + 2].reshape(256, 128), queries) for b, i in parts]
         before = m_run[:, lanes]
-        m = jnp.maximum(before, jnp.max(s, axis=0, keepdims=True))
-        p = jnp.exp2((s - m) * coef)
+        m = before
+        for s in scores:
+            m = jnp.maximum(m, jnp.max(s, axis=0, keepdims=True))
         scale = jnp.exp2((before - m) * coef)
         m_run[:, lanes] = m
-        l_run[:, lanes] = l_run[:, lanes] * scale + jnp.sum(p, axis=0, keepdims=True)
-        v_mat = jnp.concatenate([kvbuf[block, 4 + i] for i in range(4)], axis=1)
-        acc[:, lanes] = acc[:, lanes] * scale + dot(v_mat, p.astype(jnp.bfloat16))
+        summed = None
+        for (b, i), s in zip(parts, scores):
+            p = jnp.exp2((s - m) * coef).astype(jnp.bfloat16)
+            v_mat = jnp.concatenate([kvbuf[b, 4 + 2 * i], kvbuf[b, 5 + 2 * i]], axis=1)
+            part = dot(jnp.concatenate([v_mat, ones], axis=0), p)
+            summed = part if summed is None else summed + part
+        l_run[:, lanes] = l_run[:, lanes] * scale + summed[128:129]
+        acc[:, lanes] = acc[:, lanes] * scale + summed[0:128]
 
     for t in range(8):
         diagonal(t)
@@ -430,13 +502,14 @@
                     lanes = slice(i * 128, (i + 1) * 128)
                     mixed[rows, lanes] += dot(maps_ref[1, rows, :], e_mat[i]) * decay_t[rows, lanes]
 
-        ones = jnp.ones((8, 256), jnp.bfloat16)
+        ones8 = jnp.ones((8, 256), jnp.bfloat16)
+        fetches[6].wait()
         for k in range(4):
             rows = slice(k * SPAN, (k + 1) * SPAN)
             value = mixed[rows, :] * silu(gate_ref[rows, :].astype(jnp.float32))
             gated[rows, :] = value
             squares = (value * value).astype(jnp.bfloat16)
-            sq_buf[place, :, k * SPAN : (k + 1) * SPAN] = dot_t(ones, squares)
+            sq_buf[place, :, k * SPAN : (k + 1) * SPAN] = dot_t(ones8, squares)
         for d in range(1, 4):
             square_copy(d).start()
 
@@ -466,32 +539,39 @@
             square_arrival(d).wait_recv()
         total = sq_buf[0] + sq_buf[1] + sq_buf[2] + sq_buf[3]
         inv = lax.rsqrt(total * (1.0 / 1024.0) + EPSILON)
-        row8 = lax.broadcasted_iota(jnp.int32, (8, 256), 0)
-        gain = jnp.broadcast_to(gain_ref[...].reshape(1, 256), (8, 256))
-        gain = jnp.where(row8 == 0, gain, 0.0)
+        i_parts = [v[0:1] for v in parts_of(inv)]
+        g_parts = parts_of(gain_ref[...].reshape(1, 256))
+        pairs = [(0, 0), (0, 1), (1, 0), (1, 1), (0, 2), (2, 0)]
+        row16 = lax.broadcasted_iota(jnp.int32, (16, 512), 0)
+        left_rows = jnp.zeros((16, 512), jnp.float32)
+        right_rows = jnp.zeros((16, 256), jnp.float32)
+        for r, (a, b) in enumerate(pairs):
+            left_rows = jnp.where(row16 == r, i_parts[a].astype(jnp.float32), left_rows)
+            right_rows = jnp.where(row16[:, :256] == r, g_parts[b].astype(jnp.float32), right_rows)
+        right_rows = right_rows.astype(jnp.bfloat16)
         for k in range(4):
             rows = slice(k * SPAN, (k + 1) * SPAN)
-            factor = dot(inv[:, k * SPAN : (k + 1) * SPAN].T, gain, precision=HIGH)
+            factor = dot(left_rows[:, rows].T.astype(jnp.bfloat16), right_rows)
             mamba_ref[rows, :] = (gated[rows, :] * factor).astype(jnp.bfloat16)
 
     def ring(s, carry):
         for c in range(CHUNKS):
 
-            @pl.when(z >= s)
+            @pl.when(came_up(s, c))
             def _():
                 up_arrival(s, c).wait_recv()
 
-                @pl.when(jnp.logical_and(z < last, s < UP))
+                @pl.when(jnp.logical_and(z < last, s < up_hops(c)))
                 def _():
                     up_copy(s, c).start()
 
                 sib_copy(up_block(s), core * 4 + c, sib_send, sib_recv, s * CHUNKS + c).start()
 
-            @pl.when(jnp.logical_and(s <= DOWN, travels_down(s)))
+            @pl.when(travels_down(s, c))
             def _():
                 down_arrival(s, c).wait_recv()
 
-                @pl.when(s < DOWN)
+                @pl.when(s < down_hops(c))
                 def _():
                     down_copy(s, c).start()
 
@@ -505,6 +585,10 @@
                 sib_wait(s - 1)
             attend_two(s - 1, c)
 
+        @pl.when(s == STATE_STEP)
+        def _():
+            send_states()
+
         @pl.when(s == M4_STEP)
         def _():
             prefix()
@@ -516,40 +600,43 @@
         return carry
 
     def sib_wait(s):
-        @pl.when(jnp.logical_and(s >= 1, z >= s))
-        def _():
-            for c in range(CHUNKS):
+        for c in range(CHUNKS):
+
+            @pl.when(jnp.logical_and(s >= 1, came_up(s, c)))
+            def _():
                 sib_copy(
                     up_block(s), (1 - core) * 4 + c, sib_send, sib_recv, s * CHUNKS + c
                 ).wait_recv()
 
-        @pl.when(jnp.logical_and(jnp.logical_and(s >= 1, s <= DOWN), down_useful(s)))
-        def _():
-            for c in range(CHUNKS):
+            @pl.when(jnp.logical_and(s >= 1, down_useful(s, c)))
+            def _():
                 sib_copy(
                     down_block(s), (1 - core) * 4 + c, sibd_send, sibd_recv, s * CHUNKS + c
                 ).wait_recv()
 
     def attend_two(s, c):
-        @pl.when(jnp.logical_and(s >= 1, z >= s))
-        def _():
-            attend(up_block(s), 2 * c)
-            attend(up_block(s), 2 * c + 1)
-
-        @pl.when(jnp.logical_and(jnp.logical_and(s >= 1, s <= DOWN), down_useful(s)))
-        def _():
-            attend(down_block(s), 2 * c)
-            attend(down_block(s), 2 * c + 1)
-
+        up = jnp.logical_and(s >= 1, z >= s)
+        down = jnp.logical_and(s >= 1, down_useful(s, 0))
+
+        @pl.when(jnp.logical_and(up, down))
+        def _():
+            attend((up_block(s), down_block(s)), c)
+
+        @pl.when(jnp.logical_and(up, jnp.logical_not(down)))
+        def _():
+            attend((up_block(s),), c)
+
+    pl.semaphore_wait(far_sem.at[0], 2)
+    tell(1)
     lax.fori_loop(1, UP + 1, ring, 0)
+    finish_norm()
     sib_wait(UP)
 
     @pl.when(z >= UP)
     def _():
-        for t in range(8):
-            attend(up_block(UP), t)
-
-    finish_norm()
+        for t in range(4):
+            attend((up_block(UP),), t)
+
     for h in range(2):
         for i in range(4):
             lanes = slice(h * 512 + i * 128, h * 512 + (i + 1) * 128)
@@ -561,11 +648,11 @@
     def sent(s, carry):
         for c in range(CHUNKS):
 
-            @pl.when(jnp.logical_and(z >= s, z < last))
+            @pl.when(jnp.logical_and(z < last, jnp.logical_and(z >= s, s < up_hops(c))))
             def _():
                 up_copy(s, c).wait_send()
 
-            @pl.when(jnp.logical_and(s < DOWN, travels_down(s)))
+            @pl.when(jnp.logical_and(s < down_hops(c), travels_down(s, c)))
             def _():
                 down_copy(s, c).wait_send()
 
@@ -574,11 +661,11 @@
     def sent_sib(s, carry):
         for c in range(CHUNKS):
 
-            @pl.when(z >= s)
+            @pl.when(came_up(s, c))
             def _():
                 sib_copy(up_block(s), core * 4 + c, sib_send, sib_recv, s * CHUNKS + c).wait_send()
 
-            @pl.when(jnp.logical_and(s <= DOWN, down_useful(s)))
+            @pl.when(down_useful(s, c))
             def _():
                 sib_copy(
                     down_block(s), core * 4 + c, sibd_send, sibd_recv, s * CHUNKS + c
@@ -610,24 +697,29 @@
     queries,
     keys_values,
 ):
-    group = lax.axis_index("head") // 4
-    maps = lax.dynamic_index_in_dim(state_maps, group, axis=2, keepdims=False)
-    pairs = lax.dynamic_index_in_dim(keys_values, group, axis=2, keepdims=False)
-    maps = maps.transpose(1, 0, 2)
-    pairs = pairs.transpose(1, 0, 2)
     vmem = pl.BlockSpec(memory_space=pltpu.VMEM)
     smem = pl.BlockSpec(memory_space=pltpu.SMEM)
+    hbm = pl.BlockSpec(memory_space=pltpu.HBM)
     dma = pltpu.SemaphoreType.DMA
     rows = mixer_input.shape[0]
     return pl.pallas_call(
         functools.partial(kernel, n_ctx),
         out_shape=(
-            jax.ShapeDtypeStruct((rows, 256), jnp.bfloat16),
-            jax.ShapeDtypeStruct((rows, 256), jnp.bfloat16),
+            pltpu.VMEM((rows, 256), jnp.bfloat16),
+            pltpu.VMEM((rows, 256), jnp.bfloat16),
         ),
-        in_specs=[smem, smem] + [vmem] * 7,
+        in_specs=[smem, smem, vmem, vmem] + [hbm] * 5,
         out_specs=(vmem, vmem),
         scratch_shapes=[
+            pltpu.VMEM((rows, 256), jnp.bfloat16),
+            pltpu.VMEM((rows, 256), jnp.bfloat16),
+            pltpu.VMEM((rows, 256), jnp.bfloat16),
+            pltpu.VMEM((rows * 16, 128), jnp.bfloat16),
+            pltpu.VMEM((rows * 16, 128), jnp.bfloat16),
+            pltpu.VMEM((rows * 16, 128), jnp.float32),
+            pltpu.VMEM((2, rows, 128), jnp.bfloat16),
+            dma((7,)),
+            pltpu.SemaphoreType.REGULAR((2,)),
             pltpu.VMEM((n_ctx, 8, 128, 128), jnp.bfloat16),
             pltpu.VMEM((128, 1024), jnp.bfloat16),
             pltpu.VMEM((1, 1024), jnp.float32),
@@ -644,12 +736,12 @@
             pltpu.VMEM((4, 8, 512), jnp.float32),
             dma((UP * CHUNKS,)),
             dma((UP * CHUNKS,)),
-            dma((DOWN * CHUNKS,)),
-            dma((DOWN * CHUNKS,)),
+            dma((UP * CHUNKS,)),
+            dma((UP * CHUNKS,)),
             dma(((UP + 1) * CHUNKS,)),
             dma(((UP + 1) * CHUNKS,)),
-            dma(((DOWN + 1) * CHUNKS,)),
-            dma(((DOWN + 1) * CHUNKS,)),
+            dma(((UP + 1) * CHUNKS,)),
+            dma(((UP + 1) * CHUNKS,)),
             dma((n_ctx,)),
             dma((n_ctx,)),
             dma((n_ctx,)),
@@ -660,18 +752,18 @@
             dma((4,)),
         ],
         compiler_params=pltpu.CompilerParams(
-            collective_id=0, has_side_effects=True, vmem_limit_bytes=40 * 2**20
+            collective_id=0, has_side_effects=True, vmem_limit_bytes=56 * 2**20
         ),
     )(
         decay_log,
         skip_weight,
         step_raw.T,
+        norm_gain,
         mixer_input,
         gate_input,
-        maps,
-        norm_gain,
+        state_maps.reshape(rows * 16, 128),
         queries,
-        pairs,
+        keys_values.reshape(rows * 16, 128),
     )
 
 

time: 59.4 us -> 50.8 us (0.86)
  the two profiles are of different devices: /device:TPU:485 before, /device:TPU:1 now
where the time goes in v2:
time: 50.8 us; the launch traced here: 50.6 us
  Pallas kernels  48.6 us (96%)
  local copies, waits for them, and re-layouts  1.41 us (3%)
  between operations  0.64 us (1%)
    pallas_call x1, Pallas kernels, body(): pl.pallas_call(functools.partial(kernel, n_ctx), out_shape=(pltpu.VMEM((r...  48.6 us
    unnamed x2, local copies, waits for them, and re-layouts  1.41 us

profile of v2, /device:TPU:1, one launch (start us, length us, event | category | flops | bytes accessed | tf_op | source)
XLA Modules:
  0.0 50.6 jit_solution(6266250022627617066)
XLA Ops:
  0.6 48.6 %shard_map.104 = (bf16[512,256]{1,0:T(8,128)(2,1)S(1)}, bf16[512,256]{1,0:T(8,128)(2,1)S(1)}) custom-call(f32[4]{0:T(128)} %decay_ref.1, f32[4]{0:T(128)} %skip_ref.1, f32[4,512]{1,0:T(4,128)} %bitcast.5, f32[256]{0:T(256)} %gain_ref.1, bf16[512,256]{1,0:T(8,128)(2,1)} %x_hbm.1, bf16[512,256]{1,0:T(8,128)(2,1)} %gate_hbm.1, bf16[8192,128]{1,0:T(8,128)(2,1)} %bitcast.3, ...), custom_call_target="tpu_custom_call" | custom-call | tf_op jit(solution)/shard_map/pallas_call | solution.py:705
  49.2 0.7 %copy.13 = bf16[512,256]{1,0:T(8,128)(2,1)} copy(bf16[512,256]{1,0:T(8,128)(2,1)S(1)} %get-tuple-element.2) | data formatting | bytes 524288
  49.9 0.7 %copy.14 = bf16[512,256]{1,0:T(8,128)(2,1)} copy(bf16[512,256]{1,0:T(8,128)(2,1)S(1)} %get-tuple-element.3) | data formatting | bytes 524288

commit v3 on v2

--- a/solution.py
+++ b/solution.py
@@ -13,13 +13,13 @@
 NEG_FILL = -1e30
 EPSILON = 1e-5
 SPAN = 128
-CHUNKS = 4
+CHUNKS = 3
 UP = 8
-HALF = CHUNKS // 2
+DOWN_PIECE = 1
 NEAR = 2
-STATE_STEP = 1
-M4_STEP = 4
-M5_STEP = 7
+EARLY_BLOCKS = {(1, 0): (), (1, 1): (), (1, 2): (0, 1), (2, 0): (), (2, 1): (2,), (2, 2): (3,)}
+TILES = ((0, 1), (), (2, 3))
+PREFIX_AT = (4, 2)
 
 
 def softplus(v):
@@ -79,7 +79,6 @@
     acc,
     mixed,
     decay_t,
-    gated,
     total_buf,
     sbuf,
     srecv,
@@ -94,6 +93,10 @@
     sib_recv,
     sibd_send,
     sibd_recv,
+    y_send,
+    y_recv,
+    yd_send,
+    yd_recv,
     d_send,
     d_recv,
     s_send,
@@ -109,6 +112,13 @@
     sib = hd + 1 - 2 * core
     base = hd - lax.rem(hd, 4)
     place = lax.rem(hd, 4)
+    side = place // 2
+    across = base + lax.rem(place + 2, 4)
+    missing = core * 4 + 3 - 3 * side
+
+    def part(c):
+        return core * 4 + c + side * (3 - 2 * c)
+
     above = lax.rem(z + 1, n_ctx)
     below = lax.rem(z + n_ctx - 1, n_ctx)
 
@@ -148,6 +158,194 @@
     for i in range(4):
         kvbuf[z, i] = keys[i * 128 : (i + 1) * 128, :].astype(jnp.bfloat16)
         kvbuf[z, 4 + i] = values[i * 128 : (i + 1) * 128, :].T.astype(jnp.bfloat16)
+
+    def up_copy(s, c):
+        block = lax.rem(z - s + n_ctx, n_ctx)
+        return pltpu.make_async_remote_copy(
+            src_ref=kvbuf.at[block, part(c)],
+            dst_ref=kvbuf.at[block, part(c)],
+            send_sem=up_send.at[s * CHUNKS + c],
+            recv_sem=up_recv.at[s * CHUNKS + c],
+            device_id=(above, hd),
+            device_id_type=MESH,
+        )
+
+    def down_copy(s, c):
+        block = lax.rem(z + s, n_ctx)
+        return pltpu.make_async_remote_copy(
+            src_ref=kvbuf.at[block, part(c)],
+            dst_ref=kvbuf.at[block, part(c)],
+            send_sem=dn_send.at[s * CHUNKS + c],
+            recv_sem=dn_recv.at[s * CHUNKS + c],
+            device_id=(below, hd),
+            device_id_type=MESH,
+        )
+
+    def up_arrival(s, c):
+        block = lax.rem(z - s + n_ctx, n_ctx)
+        return pltpu.make_async_remote_copy(
+            src_ref=kvbuf.at[block, part(c)],
+            dst_ref=kvbuf.at[block, part(c)],
+            send_sem=up_send.at[(s - 1) * CHUNKS + c],
+            recv_sem=up_recv.at[(s - 1) * CHUNKS + c],
+            device_id=(above, hd),
+            device_id_type=MESH,
+        )
+
+    def down_arrival(s, c):
+        block = lax.rem(z + s, n_ctx)
+        return pltpu.make_async_remote_copy(
+            src_ref=kvbuf.at[block, part(c)],
+            dst_ref=kvbuf.at[block, part(c)],
+            send_sem=dn_send.at[(s - 1) * CHUNKS + c],
+            recv_sem=dn_recv.at[(s - 1) * CHUNKS + c],
+            device_id=(below, hd),
+            device_id_type=MESH,
+        )
+
+    def sib_copy(block, index, send, recv, i):
+        return pltpu.make_async_remote_copy(
+            src_ref=kvbuf.at[block, index],
+            dst_ref=kvbuf.at[block, index],
+            send_sem=send.at[i],
+            recv_sem=recv.at[i],
+            device_id=(z, sib),
+            device_id_type=MESH,
+        )
+
+    def y_copy(block, index, send, recv, i):
+        return pltpu.make_async_remote_copy(
+            src_ref=kvbuf.at[block, index],
+            dst_ref=kvbuf.at[block, index],
+            send_sem=send.at[i],
+            recv_sem=recv.at[i],
+            device_id=(z, across),
+            device_id_type=MESH,
+        )
+
+    def up_block(s):
+        return lax.rem(z - s + n_ctx, n_ctx)
+
+    def down_block(s):
+        return lax.rem(z + s, n_ctx)
+
+    def up_hops(c):
+        return UP - 1 if c == DOWN_PIECE else UP
+
+    def down_hops(c):
+        return UP if c == DOWN_PIECE else UP - 1
+
+    def came_up(s, c):
+        return jnp.logical_and(z >= s, s <= up_hops(c))
+
+    def travels_down(s, c):
+        block = lax.rem(z + s, n_ctx)
+        return jnp.logical_and(block < down_hops(c), s <= down_hops(c))
+
+    def down_useful(s, c):
+        return jnp.logical_and(z + s >= n_ctx, travels_down(s, c))
+
+    def total_copy(d):
+        return pltpu.make_async_remote_copy(
+            src_ref=total_buf.at[z],
+            dst_ref=total_buf.at[z],
+            send_sem=d_send.at[d],
+            recv_sem=d_recv.at[z],
+            device_id=(lax.rem(z + d, n_ctx), hd),
+            device_id_type=MESH,
+        )
+
+    def total_arrival(d):
+        other = lax.rem(z + d, n_ctx)
+        return pltpu.make_async_remote_copy(
+            src_ref=total_buf.at[other],
+            dst_ref=total_buf.at[other],
+            send_sem=d_send.at[d],
+            recv_sem=d_recv.at[other],
+            device_id=(other, hd),
+            device_id_type=MESH,
+        )
+
+    def state_copy(d):
+        other = lax.rem(z + d, n_ctx)
+        return pltpu.make_async_remote_copy(
+            src_ref=sbuf.at[other],
+            dst_ref=srecv.at[z],
+            send_sem=s_send.at[d],
+            recv_sem=s_recv.at[z],
+            device_id=(other, hd),
+            device_id_type=MESH,
+        )
+
+    def state_arrival(d):
+        other = lax.rem(z + d, n_ctx)
+        return pltpu.make_async_remote_copy(
+            src_ref=sbuf.at[other],
+            dst_ref=srecv.at[other],
+            send_sem=s_send.at[d],
+            recv_sem=s_recv.at[other],
+            device_id=(other, hd),
+            device_id_type=MESH,
+        )
+
+    def entering_copy(d):
+        other = lax.rem(z + d, n_ctx)
+        return pltpu.make_async_remote_copy(
+            src_ref=ebuf.at[other],
+            dst_ref=erecv.at[z],
+            send_sem=e_send.at[d],
+            recv_sem=e_recv.at[z],
+            device_id=(other, hd),
+            device_id_type=MESH,
+        )
+
+    def entering_arrival(d):
+        other = lax.rem(z + d, n_ctx)
+        return pltpu.make_async_remote_copy(
+            src_ref=ebuf.at[other],
+            dst_ref=erecv.at[other],
+            send_sem=e_send.at[d],
+            recv_sem=e_recv.at[other],
+            device_id=(other, hd),
+            device_id_type=MESH,
+        )
+
+    def each(first, last, action, cond=None):
+        def turn(d, carry):
+            if cond is None:
+                action(d)
+            else:
+
+                @pl.when(cond(d))
+                def _():
+                    action(d)
+
+            return carry
+
+        lax.fori_loop(first, last, turn, 0)
+
+    def other_of(d):
+        return lax.rem(z + d, n_ctx)
+
+    last = n_ctx - 1
+
+    pl.semaphore_wait(barrier, 2 * NEAR + 3)
+    for c in range(CHUNKS):
+
+        @pl.when(z < n_ctx - 1)
+        def _():
+            up_copy(0, c).start()
+
+        @pl.when(travels_down(0, c))
+        def _():
+            down_copy(0, c).start()
+
+    def tell(i):
+        d = NEAR * 2**i
+        for other in (lax.rem(z + d, n_ctx), lax.rem(z + n_ctx - d, n_ctx)):
+            pl.semaphore_signal(far_sem.at[i], inc=1, device_id=(other, hd), device_id_type=MESH)
+
+    tell(0)
 
     step = step_ref[...]
     raw = jnp.concatenate([step[:, k * SPAN : (k + 1) * SPAN] for k in range(4)], axis=0)
@@ -176,166 +374,6 @@
         total_rows.append(jnp.where(lane2[0:1] < 64, a, b))
     total_buf[z] = jnp.concatenate(total_rows, axis=0)
 
-    def up_copy(s, c):
-        block = lax.rem(z - s + n_ctx, n_ctx)
-        return pltpu.make_async_remote_copy(
-            src_ref=kvbuf.at[block, core * 4 + c],
-            dst_ref=kvbuf.at[block, core * 4 + c],
-            send_sem=up_send.at[s * CHUNKS + c],
-            recv_sem=up_recv.at[s * CHUNKS + c],
-            device_id=(above, hd),
-            device_id_type=MESH,
-        )
-
-    def down_copy(s, c):
-        block = lax.rem(z + s, n_ctx)
-        return pltpu.make_async_remote_copy(
-            src_ref=kvbuf.at[block, core * 4 + c],
-            dst_ref=kvbuf.at[block, core * 4 + c],
-            send_sem=dn_send.at[s * CHUNKS + c],
-            recv_sem=dn_recv.at[s * CHUNKS + c],
-            device_id=(below, hd),
-            device_id_type=MESH,
-        )
-
-    def up_arrival(s, c):
-        block = lax.rem(z - s + n_ctx, n_ctx)
-        return pltpu.make_async_remote_copy(
-            src_ref=kvbuf.at[block, core * 4 + c],
-            dst_ref=kvbuf.at[block, core * 4 + c],
-            send_sem=up_send.at[(s - 1) * CHUNKS + c],
-            recv_sem=up_recv.at[(s - 1) * CHUNKS + c],
-            device_id=(above, hd),
-            device_id_type=MESH,
-        )
-
-    def down_arrival(s, c):
-        block = lax.rem(z + s, n_ctx)
-        return pltpu.make_async_remote_copy(
-            src_ref=kvbuf.at[block, core * 4 + c],
-            dst_ref=kvbuf.at[block, core * 4 + c],
-            send_sem=dn_send.at[(s - 1) * CHUNKS + c],
-            recv_sem=dn_recv.at[(s - 1) * CHUNKS + c],
-            device_id=(below, hd),
-            device_id_type=MESH,
-        )
-
-    def sib_copy(block, part, send, recv, i):
-        return pltpu.make_async_remote_copy(
-            src_ref=kvbuf.at[block, part],
-            dst_ref=kvbuf.at[block, part],
-            send_sem=send.at[i],
-            recv_sem=recv.at[i],
-            device_id=(z, sib),
-            device_id_type=MESH,
-        )
-
-    def up_block(s):
-        return lax.rem(z - s + n_ctx, n_ctx)
-
-    def down_block(s):
-        return lax.rem(z + s, n_ctx)
-
-    def up_hops(c):
-        return UP if c < HALF else UP - 1
-
-    def down_hops(c):
-        return UP - 1 if c < HALF else UP
-
-    def came_up(s, c):
-        return jnp.logical_and(z >= s, s <= up_hops(c))
-
-    def travels_down(s, c):
-        block = lax.rem(z + s, n_ctx)
-        return jnp.logical_and(block < down_hops(c), s <= down_hops(c))
-
-    def down_useful(s, c):
-        return jnp.logical_and(z + s >= n_ctx, travels_down(s, c))
-
-    def total_copy(d):
-        return pltpu.make_async_remote_copy(
-            src_ref=total_buf.at[z],
-            dst_ref=total_buf.at[z],
-            send_sem=d_send.at[d],
-            recv_sem=d_recv.at[z],
-            device_id=(lax.rem(z + d, n_ctx), hd),
-            device_id_type=MESH,
-        )
-
-    def total_arrival(d):
-        other = lax.rem(z + d, n_ctx)
-        return pltpu.make_async_remote_copy(
-            src_ref=total_buf.at[other],
-            dst_ref=total_buf.at[other],
-            send_sem=d_send.at[d],
-            recv_sem=d_recv.at[other],
-            device_id=(other, hd),
-            device_id_type=MESH,
-        )
-
-    def state_copy(d):
-        other = lax.rem(z + d, n_ctx)
-        return pltpu.make_async_remote_copy(
-            src_ref=sbuf.at[other],
-            dst_ref=srecv.at[z],
-            send_sem=s_send.at[d],
-            recv_sem=s_recv.at[z],
-            device_id=(other, hd),
-            device_id_type=MESH,
-        )
-
-    def state_arrival(d):
-        other = lax.rem(z + d, n_ctx)
-        return pltpu.make_async_remote_copy(
-            src_ref=sbuf.at[other],
-            dst_ref=srecv.at[other],
-            send_sem=s_send.at[d],
-            recv_sem=s_recv.at[other],
-            device_id=(other, hd),
-            device_id_type=MESH,
-        )
-
-    def entering_copy(d):
-        other = lax.rem(z + d, n_ctx)
-        return pltpu.make_async_remote_copy(
-            src_ref=ebuf.at[other],
-            dst_ref=erecv.at[z],
-            send_sem=e_send.at[d],
-            recv_sem=e_recv.at[z],
-            device_id=(other, hd),
-            device_id_type=MESH,
-        )
-
-    def entering_arrival(d):
-        other = lax.rem(z + d, n_ctx)
-        return pltpu.make_async_remote_copy(
-            src_ref=ebuf.at[other],
-            dst_ref=erecv.at[other],
-            send_sem=e_send.at[d],
-            recv_sem=e_recv.at[other],
-            device_id=(other, hd),
-            device_id_type=MESH,
-        )
-
-    def each(first, last, action, cond=None):
-        def turn(d, carry):
-            if cond is None:
-                action(d)
-            else:
-
-                @pl.when(cond(d))
-                def _():
-                    action(d)
-
-            return carry
-
-        lax.fori_loop(first, last, turn, 0)
-
-    def other_of(d):
-        return lax.rem(z + d, n_ctx)
-
-    last = n_ctx - 1
-
     b_all, c_all = pick_group(maps_raw, fetches[2:4])
     maps_ref[0] = b_all.astype(jnp.bfloat16)
     maps_ref[1] = c_all.astype(jnp.bfloat16)
@@ -371,24 +409,6 @@
                 i * 128 : (i + 1) * 128, h * 128 : (h + 1) * 128
             ].T
 
-    pl.semaphore_wait(barrier, 2 * NEAR + 3)
-    for c in range(CHUNKS):
-
-        @pl.when(z < n_ctx - 1)
-        def _():
-            up_copy(0, c).start()
-
-        @pl.when(travels_down(0, c))
-        def _():
-            down_copy(0, c).start()
-
-    def tell(i):
-        d = NEAR * 2**i
-        for other in (lax.rem(z + d, n_ctx), lax.rem(z + n_ctx - d, n_ctx)):
-            pl.semaphore_signal(far_sem.at[i], inc=1, device_id=(other, hd), device_id_type=MESH)
-
-    tell(0)
-
     def send_states():
         pl.semaphore_wait(far_sem.at[1], 2)
 
@@ -403,10 +423,12 @@
     for h in range(4):
         skip = jnp.where(lane_p == h, skip_ref[h], skip)
     left = lane_w < 64
-    for k in range(4):
+    def inside_block(k):
         rows = slice(k * SPAN, (k + 1) * SPAN)
         b_mat, c_mat = maps_ref[0, rows, :], maps_ref[1, rows, :]
         scores = dot_t(c_mat, b_mat)
+        gate = silu(gate_ref[rows, :].astype(jnp.float32))
+        decay_t[rows, :] = decay_t[rows, :] * gate
         for pair in range(2):
             lanes = slice(pair * 128, (pair + 1) * 128)
             x_pair = x_ref[rows, lanes]
@@ -422,54 +444,64 @@
             )
             inside = dot(jnp.concatenate(weights, axis=1), x_two)
             total = inside + skip[:, lanes] * x_pair.astype(jnp.float32)
-            mixed[rows, lanes] = total
+            mixed[rows, lanes] = total * gate[:, lanes]
         if k > 0:
             pick = (row_r == k * 4 + head_l).astype(jnp.bfloat16)
             grown_in = jnp.exp(dot(cumul_3, jnp.concatenate([pick] * 3, axis=0)))
-            mixed[rows, :] += dot(c_mat, run_list[k - 1].astype(jnp.bfloat16)) * grown_in
+            mixed[rows, :] += dot(c_mat, run_list[k - 1].astype(jnp.bfloat16)) * (grown_in * gate)
 
     coef = math.log2(math.e) / math.sqrt(128.0)
 
-    def diagonal(t):
-        lanes = slice(t * 128, (t + 1) * 128)
-        tile = t % 4
-        count = (tile + 1) * 128
-        k_mat = kvbuf[z, 0 : tile + 1].reshape(count, 128)
-        s = dot(k_mat, qt[:, lanes])
-        key = lax.broadcasted_iota(jnp.int32, (count, 128), 0)
-        query = lax.broadcasted_iota(jnp.int32, (count, 128), 1) + tile * 128
-        s = jnp.where(key <= query, s, NEG_FILL)
-        m = jnp.max(s, axis=0, keepdims=True)
-        p = jnp.exp2((s - m) * coef)
-        m_run[:, lanes] = m
-        l_run[:, lanes] = jnp.sum(p, axis=0, keepdims=True)
-        v_mat = jnp.concatenate([kvbuf[z, 4 + i] for i in range(tile + 1)], axis=1)
-        acc[:, lanes] = dot(v_mat, p.astype(jnp.bfloat16))
+    def diagonal(tiles):
+        def scores_of(t):
+            count = (t % 4 + 1) * 128
+            s = dot(kvbuf[z, 0 : t % 4 + 1].reshape(count, 128), qt[:, t * 128 : (t + 1) * 128])
+            key = lax.broadcasted_iota(jnp.int32, (count, 128), 0)
+            query = lax.broadcasted_iota(jnp.int32, (count, 128), 1) + t % 4 * 128
+            return jnp.where(key <= query, s, NEG_FILL)
+
+        following = scores_of(tiles[0])
+        for n, t in enumerate(tiles):
+            lanes = slice(t * 128, (t + 1) * 128)
+            s = following
+            if n + 1 < len(tiles):
+                following = scores_of(tiles[n + 1])
+            m = jnp.max(s, axis=0, keepdims=True)
+            p = jnp.exp2((s - m) * coef)
+            m_run[:, lanes] = m
+            l_run[:, lanes] = jnp.sum(p, axis=0, keepdims=True)
+            v_mat = jnp.concatenate([kvbuf[z, 4 + i] for i in range(t % 4 + 1)], axis=1)
+            acc[:, lanes] = dot(v_mat, p.astype(jnp.bfloat16))
 
     ones = jnp.ones((16, 256), jnp.bfloat16)
 
-    def attend(blocks, t):
-        lanes = slice(t * 256, (t + 1) * 256)
-        queries = qt[:, lanes]
+    def attend(blocks, tiles):
         parts = [(b, i) for b in blocks for i in range(2)]
-        scores = [dot(kvbuf[b, 2 * i : 2 * i + 2].reshape(256, 128), queries) for b, i in parts]
-        before = m_run[:, lanes]
-        m = before
-        for s in scores:
-            m = jnp.maximum(m, jnp.max(s, axis=0, keepdims=True))
-        scale = jnp.exp2((before - m) * coef)
-        m_run[:, lanes] = m
-        summed = None
-        for (b, i), s in zip(parts, scores):
-            p = jnp.exp2((s - m) * coef).astype(jnp.bfloat16)
-            v_mat = jnp.concatenate([kvbuf[b, 4 + 2 * i], kvbuf[b, 5 + 2 * i]], axis=1)
-            part = dot(jnp.concatenate([v_mat, ones], axis=0), p)
-            summed = part if summed is None else summed + part
-        l_run[:, lanes] = l_run[:, lanes] * scale + summed[128:129]
-        acc[:, lanes] = acc[:, lanes] * scale + summed[0:128]
-
-    for t in range(8):
-        diagonal(t)
+        lanes_of = [slice(t * 256, (t + 1) * 256) for t in tiles]
+
+        def scores_of(lanes):
+            queries = qt[:, lanes]
+            return [dot(kvbuf[b, 2 * i : 2 * i + 2].reshape(256, 128), queries) for b, i in parts]
+
+        following = scores_of(lanes_of[0])
+        for n, lanes in enumerate(lanes_of):
+            scores = following
+            if n + 1 < len(lanes_of):
+                following = scores_of(lanes_of[n + 1])
+            before = m_run[:, lanes]
+            m = before
+            for s in scores:
+                m = jnp.maximum(m, jnp.max(s, axis=0, keepdims=True))
+            scale = jnp.exp2((before - m) * coef)
+            m_run[:, lanes] = m
+            summed = None
+            for (b, i), s in zip(parts, scores):
+                p = jnp.exp2((s - m) * coef).astype(jnp.bfloat16)
+                v_mat = jnp.concatenate([kvbuf[b, 4 + 2 * i], kvbuf[b, 5 + 2 * i]], axis=1)
+                part = dot(jnp.concatenate([v_mat, ones], axis=0), p)
+                summed = part if summed is None else summed + part
+            l_run[:, lanes] = l_run[:, lanes] * scale + summed[128:129]
+            acc[:, lanes] = acc[:, lanes] * scale + summed[0:128]
 
     def prefix():
         each(
@@ -495,21 +527,19 @@
         @pl.when(z > 0)
         def _():
             each(1, n_ctx, lambda d: entering_arrival(d).wait_recv())
-            e_mat = [erecv[i * 8 : (i + 1) * 8].reshape(128, 128) for i in range(2)]
+            e_mat = jnp.concatenate(
+                [erecv[i * 8 : (i + 1) * 8].reshape(128, 128) for i in range(2)], axis=1
+            )
             for k in range(4):
                 rows = slice(k * SPAN, (k + 1) * SPAN)
-                for i in range(2):
-                    lanes = slice(i * 128, (i + 1) * 128)
-                    mixed[rows, lanes] += dot(maps_ref[1, rows, :], e_mat[i]) * decay_t[rows, lanes]
+                mixed[rows, :] += dot(maps_ref[1, rows, :], e_mat) * decay_t[rows, :]
 
         ones8 = jnp.ones((8, 256), jnp.bfloat16)
-        fetches[6].wait()
         for k in range(4):
             rows = slice(k * SPAN, (k + 1) * SPAN)
-            value = mixed[rows, :] * silu(gate_ref[rows, :].astype(jnp.float32))
-            gated[rows, :] = value
+            value = mixed[rows, :]
             squares = (value * value).astype(jnp.bfloat16)
-            sq_buf[place, :, k * SPAN : (k + 1) * SPAN] = dot_t(ones8, squares)
+            sq_buf[place, :, rows] = dot_t(ones8, squares)
         for d in range(1, 4):
             square_copy(d).start()
 
@@ -552,9 +582,9 @@
         for k in range(4):
             rows = slice(k * SPAN, (k + 1) * SPAN)
             factor = dot(left_rows[:, rows].T.astype(jnp.bfloat16), right_rows)
-            mamba_ref[rows, :] = (gated[rows, :] * factor).astype(jnp.bfloat16)
-
-    def ring(s, carry):
+            mamba_ref[rows, :] = (mixed[rows, :] * factor).astype(jnp.bfloat16)
+
+    def ring(s, carry, early=False):
         for c in range(CHUNKS):
 
             @pl.when(came_up(s, c))
@@ -565,8 +595,6 @@
                 def _():
                     up_copy(s, c).start()
 
-                sib_copy(up_block(s), core * 4 + c, sib_send, sib_recv, s * CHUNKS + c).start()
-
             @pl.when(travels_down(s, c))
             def _():
                 down_arrival(s, c).wait_recv()
@@ -575,43 +603,69 @@
                 def _():
                     down_copy(s, c).start()
 
-                @pl.when(z + s >= n_ctx)
-                def _():
-                    sib_copy(
-                        down_block(s), core * 4 + c, sibd_send, sibd_recv, s * CHUNKS + c
-                    ).start()
-
+            @pl.when(came_up(s, c))
+            def _():
+                if c == 0:
+                    y_copy(up_block(s), part(c), y_send, y_recv, s).start()
+                sib_copy(up_block(s), part(c), sib_send, sib_recv, s * 4 + c).start()
+
+            @pl.when(down_useful(s, c))
+            def _():
+                if c == 0:
+                    y_copy(down_block(s), part(c), yd_send, yd_recv, s).start()
+                sib_copy(down_block(s), part(c), sibd_send, sibd_recv, s * 4 + c).start()
+
+            if early:
+                if s == 1:
+                    if c == 0:
+                        fetches[6].wait()
+                    if c < 2:
+                        diagonal(range(4 * c, 4 * c + 4))
+                for k in EARLY_BLOCKS[s, c]:
+                    inside_block(k)
+                if s == 2 and c == 0:
+                    send_states()
+                if s == 2 and c == 1:
+                    y_wait(1)
+                continue
             if c == 0:
-                sib_wait(s - 1)
-            attend_two(s - 1, c)
-
-        @pl.when(s == STATE_STEP)
+                sib_wait(s - 2)
+            if c == 1:
+                y_wait(s - 1)
+            if TILES[c]:
+                attend_two(s - 2, TILES[c])
+            if c == PREFIX_AT[1]:
+                pl.when(s == PREFIX_AT[0])(prefix)
+                pl.when(s == 7)(finish_mixed)
+
+        return carry
+
+    def y_wait(s):
+        @pl.when(jnp.logical_and(s >= 1, came_up(s, 0)))
         def _():
-            send_states()
-
-        @pl.when(s == M4_STEP)
+            y_copy(up_block(s), missing, y_send, y_recv, s).wait_recv()
+            sib_copy(up_block(s), missing, sib_send, sib_recv, s * 4 + 3).start()
+
+        @pl.when(jnp.logical_and(s >= 1, down_useful(s, 0)))
         def _():
-            prefix()
-
-        @pl.when(s == M5_STEP)
-        def _():
-            finish_mixed()
-
-        return carry
+            y_copy(down_block(s), missing, yd_send, yd_recv, s).wait_recv()
+            sib_copy(down_block(s), missing, sibd_send, sibd_recv, s * 4 + 3).start()
+
+    def theirs(index):
+        return index + 4 - 8 * core
 
     def sib_wait(s):
-        for c in range(CHUNKS):
-
-            @pl.when(jnp.logical_and(s >= 1, came_up(s, c)))
+        for c in range(4):
+            index, like = (missing, 0) if c == 3 else (part(c), c)
+
+            @pl.when(jnp.logical_and(s >= 1, came_up(s, like)))
+            def _():
+                sib_copy(up_block(s), theirs(index), sib_send, sib_recv, s * 4 + c).wait_recv()
+
+            @pl.when(jnp.logical_and(s >= 1, down_useful(s, like)))
             def _():
                 sib_copy(
-                    up_block(s), (1 - core) * 4 + c, sib_send, sib_recv, s * CHUNKS + c
-                ).wait_recv()
-
-            @pl.when(jnp.logical_and(s >= 1, down_useful(s, c)))
-            def _():
-                sib_copy(
-                    down_block(s), (1 - core) * 4 + c, sibd_send, sibd_recv, s * CHUNKS + c
+                    down_block(s), theirs(index), sibd_send, sibd_recv, s * 4 + c
                 ).wait_recv()
 
     def attend_two(s, c):
@@ -628,19 +682,24 @@
 
     pl.semaphore_wait(far_sem.at[0], 2)
     tell(1)
-    lax.fori_loop(1, UP + 1, ring, 0)
+    ring(1, 0, early=True)
+    ring(2, 0, early=True)
+    lax.fori_loop(3, UP + 1, ring, 0)
+    sib_wait(UP - 1)
+    attend_two(UP - 1, (0, 1))
+    y_wait(UP)
+    attend_two(UP - 1, (2, 3))
     finish_norm()
     sib_wait(UP)
 
     @pl.when(z >= UP)
     def _():
-        for t in range(4):
-            attend((up_block(UP),), t)
+        attend((up_block(UP),), (0, 1, 2, 3))
 
     for h in range(2):
         for i in range(4):
             lanes = slice(h * 512 + i * 128, h * 512 + (i + 1) * 128)
-            result = acc[:, lanes] / l_run[:, lanes]
+            result = acc[:, lanes] * (1.0 / l_run[:, lanes])
             attn_ref[i * 128 : (i + 1) * 128, h * 128 : (h + 1) * 128] = result.T.astype(
                 jnp.bfloat16
             )
@@ -658,23 +717,26 @@
 
         return carry
 
-    def sent_sib(s, carry):
-        for c in range(CHUNKS):
-
-            @pl.when(came_up(s, c))
-            def _():
-                sib_copy(up_block(s), core * 4 + c, sib_send, sib_recv, s * CHUNKS + c).wait_send()
-
-            @pl.when(down_useful(s, c))
-            def _():
-                sib_copy(
-                    down_block(s), core * 4 + c, sibd_send, sibd_recv, s * CHUNKS + c
-                ).wait_send()
+    def sent_here(s, carry):
+        for c in range(4):
+            index, like = (missing, 0) if c == 3 else (part(c), c)
+
+            @pl.when(came_up(s, like))
+            def _():
+                sib_copy(up_block(s), index, sib_send, sib_recv, s * 4 + c).wait_send()
+                if c == 0:
+                    y_copy(up_block(s), index, y_send, y_recv, s).wait_send()
+
+            @pl.when(down_useful(s, like))
+            def _():
+                sib_copy(down_block(s), index, sibd_send, sibd_recv, s * 4 + c).wait_send()
+                if c == 0:
+                    y_copy(down_block(s), index, yd_send, yd_recv, s).wait_send()
 
         return carry
 
     lax.fori_loop(0, UP, sent, 0)
-    lax.fori_loop(1, UP + 1, sent_sib, 0)
+    lax.fori_loop(1, UP + 1, sent_here, 0)
 
     @pl.when(z < last)
     def _():
@@ -727,7 +789,6 @@
             pltpu.VMEM((128, 1024), jnp.float32),
             pltpu.VMEM((512, 256), jnp.float32),
             pltpu.VMEM((512, 256), jnp.float32),
-            pltpu.VMEM((512, 256), jnp.float32),
             pltpu.VMEM((n_ctx, 2, 128), jnp.float32),
             pltpu.VMEM((n_ctx, 16, 128), jnp.bfloat16),
             pltpu.VMEM((n_ctx, 16, 128), jnp.bfloat16),
@@ -738,10 +799,14 @@
             dma((UP * CHUNKS,)),
             dma((UP * CHUNKS,)),
             dma((UP * CHUNKS,)),
-            dma(((UP + 1) * CHUNKS,)),
-            dma(((UP + 1) * CHUNKS,)),
-            dma(((UP + 1) * CHUNKS,)),
-            dma(((UP + 1) * CHUNKS,)),
+            dma(((UP + 1) * 4,)),
+            dma(((UP + 1) * 4,)),
+            dma(((UP + 1) * 4,)),
+            dma(((UP + 1) * 4,)),
+            dma((UP + 1,)),
+            dma((UP + 1,)),
+            dma((UP + 1,)),
+            dma((UP + 1,)),
             dma((n_ctx,)),
             dma((n_ctx,)),
             dma((n_ctx,)),

time: 50.8 us -> 47.3 us (0.931)
  Pallas kernels: 48.6 us -> 45 us
    pallas_call x1, Pallas kernels: 48.6 us -> 45 us  [body(): pl.pallas_call(functools.partial(kernel, n_ctx), out_shape=(pltpu.VMEM((r...]
where the time goes in v3:
time: 47.3 us; the launch traced here: 47.1 us
  Pallas kernels  45 us (95%)
  local copies, waits for them, and re-layouts  1.41 us (3%)
  between operations  0.64 us (1%)
    pallas_call x1, Pallas kernels, body(): pl.pallas_call(functools.partial(kernel, n_ctx), out_shape=(pltpu.VMEM((r...  45 us
    unnamed x2, local copies, waits for them, and re-layouts  1.41 us

profile of v3, /device:TPU:1, one launch (start us, length us, event | category | flops | bytes accessed | tf_op | source)
XLA Modules:
  0.0 47.1 jit_solution(4259956500642129792)
XLA Ops:
  0.6 45.0 %shard_map.104 = (bf16[512,256]{1,0:T(8,128)(2,1)S(1)}, bf16[512,256]{1,0:T(8,128)(2,1)S(1)}) custom-call(f32[4]{0:T(128)} %decay_ref.1, f32[4]{0:T(128)} %skip_ref.1, f32[4,512]{1,0:T(4,128)} %bitcast.5, f32[256]{0:T(256)} %gain_ref.1, bf16[512,256]{1,0:T(8,128)(2,1)} %x_hbm.1, bf16[512,256]{1,0:T(8,128)(2,1)} %gate_hbm.1, bf16[8192,128]{1,0:T(8,128)(2,1)} %bitcast.3, ...), custom_call_target="tpu_custom_call" | custom-call | tf_op jit(solution)/shard_map/pallas_call | solution.py:767
  45.7 0.7 %copy.13 = bf16[512,256]{1,0:T(8,128)(2,1)} copy(bf16[512,256]{1,0:T(8,128)(2,1)S(1)} %get-tuple-element.2) | data formatting | bytes 524288
  46.4 0.7 %copy.14 = bf16[512,256]{1,0:T(8,128)(2,1)} copy(bf16[512,256]{1,0:T(8,128)(2,1)S(1)} %get-tuple-element.3) | data formatting | bytes 524288

commit v4 on v3

--- a/solution.py
+++ b/solution.py
@@ -623,7 +623,7 @@
                         diagonal(range(4 * c, 4 * c + 4))
                 for k in EARLY_BLOCKS[s, c]:
                     inside_block(k)
-                if s == 2 and c == 0:
+                if s == 2 and c == 2:
                     send_states()
                 if s == 2 and c == 1:
                     y_wait(1)
@@ -636,7 +636,7 @@
                 attend_two(s - 2, TILES[c])
             if c == PREFIX_AT[1]:
                 pl.when(s == PREFIX_AT[0])(prefix)
-                pl.when(s == 7)(finish_mixed)
+                pl.when(s == jnp.where(z == 0, 4, 7))(finish_mixed)
 
         return carry
 

time: 47.3 us -> 45.4 us (0.960)
  the two profiles are of different devices: /device:TPU:1 before, /device:TPU:35 now
where the time goes in v4:
time: 45.4 us; the launch traced here: 45.2 us
  Pallas kernels  43.2 us (95%)
  local copies, waits for them, and re-layouts  1.41 us (3%)
  between operations  0.64 us (1%)
    pallas_call x1, Pallas kernels, body(): pl.pallas_call(functools.partial(kernel, n_ctx), out_shape=(pltpu.VMEM((r...  43.2 us
    unnamed x2, local copies, waits for them, and re-layouts  1.41 us

profile of v4, /device:TPU:35, one launch (start us, length us, event | category | flops | bytes accessed | tf_op | source)
XLA Modules:
  0.0 45.2 jit_solution(10802339341556621628)
XLA Ops:
  0.6 43.2 %shard_map.104 = (bf16[512,256]{1,0:T(8,128)(2,1)S(1)}, bf16[512,256]{1,0:T(8,128)(2,1)S(1)}) custom-call(f32[4]{0:T(128)} %decay_ref.1, f32[4]{0:T(128)} %skip_ref.1, f32[4,512]{1,0:T(4,128)} %bitcast.5, f32[256]{0:T(256)} %gain_ref.1, bf16[512,256]{1,0:T(8,128)(2,1)} %x_hbm.1, bf16[512,256]{1,0:T(8,128)(2,1)} %gate_hbm.1, bf16[8192,128]{1,0:T(8,128)(2,1)} %bitcast.3, ...), custom_call_target="tpu_custom_call" | custom-call | tf_op jit(solution)/shard_map/pallas_call | solution.py:767
  43.8 0.7 %copy.13 = bf16[512,256]{1,0:T(8,128)(2,1)} copy(bf16[512,256]{1,0:T(8,128)(2,1)S(1)} %get-tuple-element.2) | data formatting | bytes 524288
  44.5 0.7 %copy.14 = bf16[512,256]{1,0:T(8,128)(2,1)} copy(bf16[512,256]{1,0:T(8,128)(2,1)S(1)} %get-tuple-element.3) | data formatting | bytes 524288

commit v5 on v4

--- a/solution.py
+++ b/solution.py
@@ -778,7 +778,7 @@
             pltpu.VMEM((rows, 256), jnp.bfloat16),
             pltpu.VMEM((rows * 16, 128), jnp.bfloat16),
             pltpu.VMEM((rows * 16, 128), jnp.bfloat16),
-            pltpu.VMEM((rows * 16, 128), jnp.float32),
+            pltpu.VMEM((rows * 16 + 16, 128), jnp.float32),
             pltpu.VMEM((2, rows, 128), jnp.bfloat16),
             dma((7,)),
             pltpu.SemaphoreType.REGULAR((2,)),

time: 45.4 us -> 45.4 us (level)
  no operation moved by 1% of the time
where the time goes in v5:
time: 45.4 us; the launch traced here: 45.2 us
  Pallas kernels  43.1 us (95%)
  local copies, waits for them, and re-layouts  1.41 us (3%)
  between operations  0.64 us (1%)
    pallas_call x1, Pallas kernels, body(): pl.pallas_call(functools.partial(kernel, n_ctx), out_shape=(pltpu.VMEM((r...  43.1 us
    unnamed x2, local copies, waits for them, and re-layouts  1.41 us

profile of v5, /device:TPU:35, one launch (start us, length us, event | category | flops | bytes accessed | tf_op | source)
XLA Modules:
  0.0 45.2 jit_solution(10239243124802886592)
XLA Ops:
  0.6 43.1 %shard_map.104 = (bf16[512,256]{1,0:T(8,128)(2,1)S(1)}, bf16[512,256]{1,0:T(8,128)(2,1)S(1)}) custom-call(f32[4]{0:T(128)} %decay_ref.1, f32[4]{0:T(128)} %skip_ref.1, f32[4,512]{1,0:T(4,128)} %bitcast.5, f32[256]{0:T(256)} %gain_ref.1, bf16[512,256]{1,0:T(8,128)(2,1)} %x_hbm.1, bf16[512,256]{1,0:T(8,128)(2,1)} %gate_hbm.1, bf16[8192,128]{1,0:T(8,128)(2,1)} %bitcast.3, ...), custom_call_target="tpu_custom_call" | custom-call | tf_op jit(solution)/shard_map/pallas_call | solution.py:767
  43.8 0.7 %copy.13 = bf16[512,256]{1,0:T(8,128)(2,1)} copy(bf16[512,256]{1,0:T(8,128)(2,1)S(1)} %get-tuple-element.2) | data formatting | bytes 524288
  44.5 0.7 %copy.14 = bf16[512,256]{1,0:T(8,128)(2,1)} copy(bf16[512,256]{1,0:T(8,128)(2,1)S(1)} %get-tuple-element.3) | data formatting | bytes 524288
